TPU v7x, 512 devices: a whole 4x4x16 slice. The times are simulated.
512 devices in a mesh: group: 8 (over y, core), cluster: 64 (over z, x).
Axes of the slice: x: 4, y: 4, z: 16, core: 2. Of those that a mesh axis runs over, the one named last changes fastest.
Arguments:
- queries: bfloat16 [57344, 4096], P(('group', 'cluster')), may hold values from -128 to 128
- cluster_id: int32 [57344, 1], P(('group', 'cluster')), may hold values from 0 to 63; in each aligned block of 112 rows (0 to 111, 112 to 223, ...) at most 4 rows name the same one
- block_list: int32 [57344, 2], P(('group', 'cluster')), may hold values from 0 to 2, all different within a row
- positive: int32 [57344], P(('group', 'cluster')), may hold values from 0 to 63
- passages: bfloat16 [98304, 4096], P(('group', 'cluster')), may hold values from -6 to 6
- pool_rows: bfloat16 [128, 4096], P('cluster'), may hold values from -5 to 5
- logit_scale: float32 [1], replicated, may hold values from 0.5 to 2
Outputs:
- query_grad: bfloat16 [57344, 4096], P(('group', 'cluster'))
- passage_grad: bfloat16 [98304, 4096], P(('group', 'cluster'))
- pool_grad: float32 [128, 4096], P('cluster')
- loss: float32 [1], replicated
- scale_grad: float32 [1], replicated
Inputs may be any that keep to these rules, and one draw needn't show every extreme that they name: `cluster_id`: of the 112 queries of one device at most 4 name the same cluster, and in some device exactly 4 do; every cluster is named by some query. `block_list`: each row names 2 different blocks.
All inputs are finite; a program needn't handle non-finite values.
Results may differ from a plain program's by a relative error of at most 0.0095.
Values may be sent and summed in bfloat16 or wider, within the bound.
A program may use at most 64 MiB of HBM per device.

v0:
```python
import math

import jax
import jax.numpy as jnp
from jax import lax
from jax.sharding import PartitionSpec as P

BLOCK = 64


def owner_pass(routed, blocks, positive_col, live_rows, local_rows, pool_all, logit_scale):
    model_width = routed.shape[1]
    inv_root = 1.0 / math.sqrt(model_width)
    factor = logit_scale[0] * inv_root
    contract = (((1,), (1,)), ((), ()))
    raw_blk = lax.dot_general(routed, local_rows, contract, preferred_element_type=jnp.float32)
    raw_pool = lax.dot_general(routed, pool_all, contract, preferred_element_type=jnp.float32)
    score_blk = factor * raw_blk
    score_pool = factor * raw_pool
    block_count = local_rows.shape[0] // BLOCK
    block_ok = jnp.any(
        blocks[:, :, None] == jnp.arange(block_count, dtype=jnp.int32)[None, None, :], axis=1
    )
    allowed = jnp.repeat(block_ok, BLOCK, axis=1)
    peak_score = jnp.maximum(
        jnp.max(jnp.where(allowed, score_blk, -jnp.inf), axis=1), jnp.max(score_pool, axis=1)
    )
    exp_blk = jnp.where(allowed, jnp.exp(score_blk - peak_score[:, None]), 0.0)
    exp_pool = jnp.exp(score_pool - peak_score[:, None])
    row_total = jnp.sum(exp_blk, axis=1) + jnp.sum(exp_pool, axis=1)
    log_total = peak_score + jnp.log(row_total)
    target = blocks[:, 0] * BLOCK + positive_col
    target_hit = jnp.arange(local_rows.shape[0], dtype=jnp.int32)[None, :] == target[:, None]
    score_pos = jnp.sum(jnp.where(target_hit, score_blk, 0.0), axis=1)
    weight = live_rows.astype(jnp.float32)
    loss_part = jnp.sum(weight * (log_total - score_pos))
    grad_blk = weight[:, None] * (exp_blk / row_total[:, None] - target_hit.astype(jnp.float32))
    grad_pool = weight[:, None] * (exp_pool / row_total[:, None])
    scale_part = inv_root * (jnp.sum(grad_blk * raw_blk) + jnp.sum(grad_pool * raw_pool))
    low_blk = grad_blk.astype(jnp.bfloat16)
    low_pool = grad_pool.astype(jnp.bfloat16)
    query_grad = (
        factor
        * (
            jnp.dot(low_blk, local_rows, preferred_element_type=jnp.float32)
            + jnp.dot(low_pool, pool_all, preferred_element_type=jnp.float32)
        )
    ).astype(jnp.bfloat16)
    passage_grad = (
        factor
        * lax.dot_general(
            low_blk, routed, (((0,), (0,)), ((), ())), preferred_element_type=jnp.float32
        )
    ).astype(jnp.bfloat16)
    return (loss_part, scale_part, query_grad, passage_grad, low_pool, factor)


def per_device(queries, cluster_id, block_list, positive, passages, pool_rows, logit_scale):
    query_count = queries.shape[0]
    model_width = queries.shape[1]
    owners = lax.axis_size("cluster")
    capacity = max(4, 2 * query_count // owners)
    slots = owners * capacity
    kcount = block_list.shape[1]
    cluster_of = cluster_id[:, 0]
    onehot = (cluster_of[:, None] == jnp.arange(owners, dtype=jnp.int32)[None, :]).astype(jnp.int32)
    slot_rank = jnp.sum((jnp.cumsum(onehot, axis=0) - onehot) * onehot, axis=1)
    slot_of = cluster_of * capacity + slot_rank
    picker = jnp.arange(slots, dtype=jnp.int32)[:, None] == slot_of[None, :]
    row_meta = jnp.concatenate(
        [block_list, positive[:, None], jnp.ones((query_count, 1), jnp.int32)], axis=1
    )
    send_rows = jnp.dot(
        picker.astype(jnp.bfloat16), queries, preferred_element_type=jnp.float32
    ).astype(jnp.bfloat16)
    send_meta = jnp.dot(picker.astype(jnp.int32), row_meta)
    routed, routed_meta = (
        lax.all_to_all(
            send_rows.reshape(owners, capacity, model_width),
            "cluster",
            split_axis=0,
            concat_axis=0,
            tiled=True,
        ),
        lax.all_to_all(
            send_meta.reshape(owners, capacity, kcount + 2),
            "cluster",
            split_axis=0,
            concat_axis=0,
            tiled=True,
        ),
    )
    routed = routed.reshape(slots, model_width)
    routed_meta = routed_meta.reshape(slots, kcount + 2)
    pool_all = lax.all_gather(pool_rows, "cluster", axis=0, tiled=True)
    loss_part, scale_part, query_part, passage_grad, low_pool, factor = owner_pass(
        routed,
        routed_meta[:, :kcount],
        routed_meta[:, kcount],
        routed_meta[:, kcount + 1] > 0,
        passages,
        pool_all,
        logit_scale,
    )
    returned = lax.all_to_all(
        query_part.reshape(owners, capacity, model_width),
        "cluster",
        split_axis=0,
        concat_axis=0,
        tiled=True,
    )
    home_grad = lax.dot_general(
        picker.astype(jnp.bfloat16),
        returned.reshape(slots, model_width),
        (((0,), (0,)), ((), ())),
        preferred_element_type=jnp.float32,
    ).astype(jnp.bfloat16)
    pick_rows = pool_rows.shape[0]
    pool_term = factor * lax.dot_general(
        low_pool, routed, (((0,), (0,)), ((), ())), preferred_element_type=jnp.float32
    )
    summed = lax.psum(pool_term, ("group", "cluster"))
    pool_grad = lax.dynamic_slice_in_dim(
        summed, lax.axis_index("cluster") * pick_rows, pick_rows, 0
    )
    loss_total, scale_grad = lax.psum((loss_part, scale_part), ("group", "cluster"))
    query_total = lax.axis_size("group") * owners * query_count
    return (
        home_grad,
        passage_grad,
        pool_grad,
        (loss_total / query_total).reshape(1),
        scale_grad.reshape(1),
    )


def solution(mesh):
    placed = (
        P(("group", "cluster"), None),
        P(("group", "cluster"), None),
        P(("group", "cluster"), None),
        P(("group", "cluster")),
        P(("group", "cluster"), None),
        P("cluster", None),
        P(),
    )
    return jax.shard_map(
        per_device,
        mesh=mesh,
        in_specs=placed,
        out_specs=(
            P(("group", "cluster"), None),
            P(("group", "cluster"), None),
            P("cluster", None),
            P(),
            P(),
        ),
        check_vma=False,
    )
```

profile of v0, /device:TPU:1, one launch (start us, length us, event | category | flops | bytes accessed | tf_op | source)
XLA Modules:
  0.0 766.1 jit_solution(15535616377575822304)
XLA Ops:
  7.2 0.0 copy-start
  7.2 0.9 fusion.12
  8.0 0.1 pad.2.clone
  8.1 0.2 reduce_window_sum.11
  8.3 0.8 select_reduce_fusion.1
  9.1 0.7 multiply_add_fusion
  9.8 0.9 fusion.5
  10.7 0.2 reshape.60
  10.8 0.7 copy.17
  11.6 19.1 %all-to-all-start = ((s32[64,4,4]{1,2,0:T(4,128)}), s32[64,4,4]{1,2,0:T(4,128)S(1)}, u32[]{:S(2)}, u32[]{:S(2)}) async-start(s32[64,4,4]{1,2,0:T(4,128)} %copy.17), calls=%async_computation | async-start | bytes 262144 | tf_op jit(solution)/shard_map/all_to_all | solution.py:85
  30.7 3.2 convolution_convert_fusion
  33.9 4.1 reshape.63
  38.1 7.6 all-to-all-done
  45.6 7.2 all-to-all-start.1
  52.9 0.0 all-gather.3.cloned.1.call-start
  52.9 0.7 all-gather.3.cloned.1.call-update
  54.3 0.1 reshape.61
  54.4 152.9 %all-gather.3.cloned.1.call-done = bf16[64,2,4096]{2,1,0:T(2,128)(2,1)} async-done(((bf16[1,2,4096]{2,1,0:T(2,128)(2,1)}), bf16[64,2,4096]{2,1,0:T(2,128)(2,1)}) %all-gather.3.cloned.1.call-update) | async-done | bytes 1048592 | tf_op jit(solution)/shard_map/all_gather | solution.py:95
  207.4 1.5 reshape.70
  208.8 0.0 all-to-all-done.1
  208.8 4.0 reshape.64
  212.8 0.0 copy-start.1
  212.8 2.6 multiply_reduce_fusion.2
  215.4 0.0 copy-done
  215.4 0.0 copy-done.1
  215.4 0.9 fusion.3
  216.4 0.1 fusion.4
  216.4 0.7 fusion.21
  217.2 0.7 multiply_reduce_fusion
  217.9 2.1 fusion.1
  220.0 4.1 reshape.65
  224.1 9.3 %all-to-all-start.2 = ((bf16[64,4,4096]{2,1,0:T(4,128)(2,1)}), bf16[64,4,4096]{2,1,0:T(4,128)(2,1)}, u32[]{:S(2)}, u32[]{:S(2)}) async-start(bf16[64,4,4096]{2,1,0:T(4,128)(2,1)} %reshape.65), calls=%async_computation.2 | async-start | bytes 4194304 | tf_op jit(solution)/shard_map/all_to_all | solution.py:105
  233.4 0.0 all-reduce.3.cloned.1.call-start
  233.5 3.4 convolution_multiply_fusion.1
  236.9 0.0 all-reduce.3.cloned.1.call-update
  236.9 0.6 multiply_reduce_fusion.1
  238.9 0.6 select_reduce_fusion.2
  239.5 161.9 %all-reduce = (f32[]{:T(128)}, f32[1]{0:T(128)}) all-reduce(f32[]{:T(128)} %select_reduce_fusion.2, f32[1]{0:T(128)} %bitcast.7), channel_id=1, replica_groups=mesh['group'=8,'cluster'=64] {'group','cluster'}, use_global_device_ids=true, to_apply=%region_10.11 | all-reduce | flops 2 | bytes 16 | tf_op jit(solution)/shard_map/psum | solution.py:126
  402.0 3.3 fusion.2
  405.3 344.3 %all-reduce.3.cloned.1.call-done = f32[128,4096]{1,0:T(8,128)} async-done(((f32[128,4096]{1,0:T(8,128)}), f32[128,4096]{1,0:T(8,128)}) %all-reduce.3.cloned.1.call-update) | async-done | bytes 2097168 | tf_op jit(solution)/shard_map/psum | solution.py:122
  749.7 1.5 constant_dynamic-slice_fusion
  751.2 0.0 all-to-all-done.2
  751.2 4.0 reshape.66
  755.2 3.0 convolution_convert_fusion.1
  (9 shorter events, 0.1 us)
Async XLA Ops:
  7.2 208.2 %copy-start = (bf16[192,4096]{1,0:T(8,128)(2,1)S(1)}, bf16[192,4096]{1,0:T(8,128)(2,1)}, u32[]{:S(2)}) copy-start(bf16[192,4096]{1,0:T(8,128)(2,1)} %param.11) | copy-start | bytes 4718596
  11.6 34.0 %all-to-all-start = ((s32[64,4,4]{1,2,0:T(4,128)}), s32[64,4,4]{1,2,0:T(4,128)S(1)}, u32[]{:S(2)}, u32[]{:S(2)}) async-start(s32[64,4,4]{1,2,0:T(4,128)} %copy.17), calls=%async_computation | async-start | bytes 262144 | tf_op jit(solution)/shard_map/all_to_all | solution.py:85
  45.6 163.2 %all-to-all-start.1 = ((bf16[64,4,4096]{2,1,0:T(4,128)(2,1)}), bf16[64,4,4096]{2,1,0:T(4,128)(2,1)}, u32[]{:S(2)}, u32[]{:S(2)}) async-start(bf16[64,4,4096]{2,1,0:T(4,128)(2,1)} %reshape.63), calls=%async_computation.1 | async-start | bytes 4194304 | tf_op jit(solution)/shard_map/all_to_all | solution.py:78
  52.9 154.5 %all-gather.3.cloned.1.call-start = ((), (), s32[]{:S(2)}) async-start(), calls=%async_computation.4 | async-start | bytes 1064960 | tf_op jit(solution)/shard_map/all_gather | solution.py:95
  212.8 2.6 copy-start.1
  224.1 527.1 %all-to-all-start.2 = ((bf16[64,4,4096]{2,1,0:T(4,128)(2,1)}), bf16[64,4,4096]{2,1,0:T(4,128)(2,1)}, u32[]{:S(2)}, u32[]{:S(2)}) async-start(bf16[64,4,4096]{2,1,0:T(4,128)(2,1)} %reshape.65), calls=%async_computation.2 | async-start | bytes 4194304 | tf_op jit(solution)/shard_map/all_to_all | solution.py:105
  233.4 516.2 %all-reduce.3.cloned.1.call-start = ((), (), s32[]{:S(2)}) async-start(), calls=%async_computation.3 | async-start | bytes 4194304 | tf_op jit(solution)/shard_map/psum | solution.py:122
Sparse Core Ops, SparseCore 0:
  56.6 150.6 all-gather.2
  239.6 509.9 all-reduce.2
where the time goes:
time: 767 us; the launch traced here: 766 us
  waiting for transfers between devices  506 us (66%)
  blocking collectives  162 us (21%)
  starting transfers between devices  35.7 us (5%)
  local copies, waits for them, and re-layouts  20.3 us (3%)
  matrix products  20.2 us (3%)
  between operations  17.9 us (2%)
    psum x1, waiting for transfers between devices, per_device(): summed = lax.psum(pool_term, ('group', 'cluster'))  344 us
    psum x1, blocking collectives, per_device(): lax.psum((loss_part, scale_part), ('group', 'cluster'))  162 us
    all_gather x1, waiting for transfers between devices, per_device(): pool_all = lax.all_gather(pool_rows, 'cluster', axis=0, tiled=True)  153 us
    all_to_all x1, starting transfers between devices, per_device(): lax.all_to_all(send_meta.reshape(owners, capacity, kcount + 2), 'cluster'...  19.1 us
  transfers between devices with their start and end apart: 5, of which 3 were waited for; matrix products, arithmetic and copies ran while one was open for 2% of the time, Pallas kernels for 0%

commit v1 on v0

v1 whole, which is shorter than its diff:
```python
import math

import jax
import jax.numpy as jnp
from jax import lax
from jax.experimental import pallas as pl
from jax.experimental.pallas import tpu as pltpu
from jax.sharding import PartitionSpec as P

D = 4096
TQ = 112
BLOCK = 64
TP = 192
POOL = 128
NX = 4
NZ = 16
NY = 4
OWNERS = NX * NZ
CAP = 4
CHUNKS = 4
PER = OWNERS // CHUNKS
SLOTS = PER * CAP
W = D // 4
INV_ROOT = 1.0 / math.sqrt(D)
MESH = pl.DeviceIdType.MESH
F32 = jnp.float32
BF16 = jnp.bfloat16


def iota(shape, axis):
    return lax.broadcasted_iota(jnp.int32, shape, axis)


def onehot(mask):
    return jnp.where(mask, 1.0, 0.0).astype(BF16)


def kernel(
    q_ref, cl_ref, bl_ref, pos_ref, p_ref, piece_ref, scale_ref,
    home_ref, pg_ref, poolg_ref, loss_ref, sgrad_ref,
    snd, rcv, msnd, mrcv, gsnd, grcv, stack, routed, low, lowt, acc, gp, pool,
    pt, rc, s1, ry, s2, rx, zb, rz, fin, gb, sc, rcs, rys, rxs,
    d_send, d_recv, m_send, m_recv, g_send, g_recv, p_send, p_recv, r_send, r_recv, t_send, t_recv,
):
    grp = lax.axis_index("group")
    clu = lax.axis_index("cluster")
    y, core = grp // 2, grp % 2
    z, x = clu // NX, clu % NX

    def cluster_peer(dz, dx):
        return (grp, ((z + dz + NZ) % NZ) * NX + (x + dx + NX) % NX)

    def group_peer(py, pc):
        return (py * 2 + pc, clu)

    def offset(o):
        return ((o // 4) % 4) * 4 + o // 16, o % 4

    def copy(src, dst, send, recv, peer):
        return pltpu.make_async_remote_copy(
            src_ref=src, dst_ref=dst, send_sem=send, recv_sem=recv, device_id=peer, device_id_type=MESH
        )

    here = (grp, clu)
    barrier = pltpu.get_barrier_semaphore()

    def greet(o, carry):
        dz, dx = offset(o)
        pl.semaphore_signal(barrier, inc=1, device_id=cluster_peer(dz, dx), device_id_type=MESH)
        return carry

    lax.fori_loop(1, OWNERS, greet, 0)

    def greet_group(k, carry):
        pl.semaphore_signal(barrier, inc=1, device_id=((grp + k) % 8, clu), device_id_type=MESH)
        return carry

    lax.fori_loop(1, 8, greet_group, 0)

    factor = scale_ref[0] * INV_ROOT

    a_iota, b_iota = iota((TQ, TQ), 0), iota((TQ, TQ), 1)
    eye = a_iota == b_iota

    def to_col(row):
        return jnp.sum(jnp.where(eye, row.astype(F32), 0.0), axis=1, keepdims=True)

    cl_row = cl_ref[...]
    cl_col = to_col(cl_row).astype(jnp.int32)
    same = cl_col == cl_row
    rank_row = jnp.sum(jnp.where(same & (a_iota < b_iota), 1.0, 0.0), axis=0, keepdims=True).astype(jnp.int32)
    rank_col = jnp.sum(jnp.where(same & (b_iota < a_iota), 1.0, 0.0), axis=1, keepdims=True).astype(jnp.int32)

    def offset_of(cl):
        dz = ((cl >> 2) - z) & 15
        return (dz & 3) * 16 + (dz >> 2) * 4 + ((cl - x) & 3)

    off_row, off_col = offset_of(cl_row), offset_of(cl_col)
    place_row = off_row * 16 + rank_row
    place_col = off_col * 16 + rank_col

    lane = iota((TQ, 128), 1)
    field = lane >> 2
    block0, block1, position = to_col(bl_ref[0:1, :]), to_col(bl_ref[1:2, :]), to_col(pos_ref[...])
    value = jnp.where(field == 0, block0, jnp.where(field == 1, block1, jnp.where(field == 2, position, 1.0)))
    value = jnp.where((rank_col == (lane & 3)) & (field < 4), value, 0.0).astype(BF16)
    meta = jnp.dot(onehot(iota((OWNERS, TQ), 0) == off_row), value, preferred_element_type=F32)
    msnd[:, 0, :] = meta

    def build(c, carry):
        row = iota((PER * 16, TQ), 0) + c * (PER * 16)
        total = jnp.zeros((PER * 16, W), F32)
        for b in range(4):
            pick = onehot(row == place_row + 4 * b)
            total = total + jnp.dot(pick, q_ref[:, b * W:(b + 1) * W], preferred_element_type=F32)
        snd[pl.ds(c * PER, PER)] = total.astype(BF16).reshape(PER, 16, W)
        return carry

    def send_chunk(c):
        def step(o, carry):
            dz, dx = offset(o)
            peer = cluster_peer(dz, dx)
            copy(msnd.at[o], mrcv.at[o], m_send, m_recv.at[o // PER], peer).start()
            copy(snd.at[o], rcv.at[o], d_send, d_recv.at[o // PER], peer).start()
            return carry

        lax.fori_loop(1 if c == 0 else c * PER, (c + 1) * PER, step, 0)

    build(0, 0)
    gp[y, x, z] = piece_ref[y]
    pl.semaphore_wait(barrier, OWNERS - 1 + 7)

    def pool_z(k, carry):
        copy(gp.at[y, x, z], gp.at[y, x, z], p_send.at[0], p_recv.at[0], cluster_peer(k, 0)).start()
        return carry

    lax.fori_loop(1, NZ, pool_z, 0)
    for c in range(CHUNKS):
        send_chunk(c)
        if c + 1 < CHUNKS:
            build(c + 1, 0)
    rcv[0] = snd[0]
    mrcv[0] = msnd[0]

    some = gp.at[y, x, pl.ds(0, NZ - 1)]
    copy(some, some, p_send.at[0], p_recv.at[0], here).wait()
    for k in range(1, NX):
        copy(gp.at[y, x], gp.at[y, x], p_send.at[1], p_recv.at[1], cluster_peer(0, k)).start()
    some = gp.at[y, pl.ds(0, NX - 1)]
    copy(some, some, p_send.at[1], p_recv.at[1], here).wait()
    for k in range(1, NY):
        copy(gp.at[y], gp.at[y], p_send.at[2], p_recv.at[2], group_peer((y + k) % NY, core)).start()
    some = gp.at[pl.ds(0, NY - 1)]
    copy(some, some, p_send.at[2], p_recv.at[2], here).wait()

    def spread(yy, carry):
        flat = gp[yy].reshape(OWNERS * 16, 128)
        i, j = iota((POOL, OWNERS * 16), 0), iota((POOL, OWNERS * 16), 1)
        base = (i >> 5) * (NZ * 16) + (i & 15) * 16 + ((i >> 4) & 1) * 8
        for cb in range(8):
            part = jnp.dot(onehot(j == base + cb), flat, preferred_element_type=F32).astype(BF16)
            pool[:, pl.ds(pl.multiple_of(yy * W + cb * 128, 128), 128)] = part
        return carry

    lax.fori_loop(0, NY, spread, 0)

    i, j = iota((256, 256), 0), iota((256, 256), 1)
    unmix = onehot(((i >> 2) & 15) * 16 + (i >> 6) * 4 + (i & 3) == j)
    mix = onehot(((j >> 2) & 15) * 16 + (j >> 6) * 4 + (j & 3) == i)
    contract = (((1,), (1,)), ((), ()))

    def work(c, carry):
        loss_sum, scale_sum = carry
        some = rcv.at[pl.ds(c * PER, PER)]
        rows = rcv[pl.ds(c * PER, PER)].reshape(PER * 16, W)
        plain = jnp.dot(unmix, rows, preferred_element_type=F32).astype(BF16)
        for b in range(4):
            routed[pl.ds(c * SLOTS, SLOTS), b * W:(b + 1) * W] = plain[b * SLOTS:(b + 1) * SLOTS]
        mine = routed[pl.ds(c * SLOTS, SLOTS), :]
        raw_blk = lax.dot_general(mine, p_ref[...], contract, preferred_element_type=F32)
        raw_pool = lax.dot_general(mine, pool[...], contract, preferred_element_type=F32)
        expand = onehot((iota((SLOTS, PER), 0) >> 2) == iota((SLOTS, PER), 1))
        got = mrcv[pl.ds(c * PER, PER), 0, :].astype(BF16)
        got = jnp.dot(expand, got, preferred_element_type=F32)
        lanes, rank = iota((SLOTS, 128), 1), iota((SLOTS, 128), 0) & 3

        def column(f):
            return jnp.sum(jnp.where(lanes == 4 * f + rank, got, 0.0), axis=1, keepdims=True)

        first, second, place, weight = column(0), column(1), column(2), column(3)
        cand = iota((SLOTS, TP), 1)
        block = (cand >> 6).astype(F32)
        allowed = (block == first) | (block == second)
        hit = cand.astype(F32) == first * BLOCK + place
        score_blk = factor * raw_blk
        score_pool = factor * raw_pool
        peak = jnp.maximum(
            jnp.max(jnp.where(allowed, score_blk, -jnp.inf), axis=1, keepdims=True),
            jnp.max(score_pool, axis=1, keepdims=True),
        )
        exp_blk = jnp.where(allowed, jnp.exp(jnp.where(allowed, score_blk - peak, 0.0)), 0.0)
        exp_pool = jnp.exp(score_pool - peak)
        total = jnp.sum(exp_blk, axis=1, keepdims=True) + jnp.sum(exp_pool, axis=1, keepdims=True)
        log_total = peak + jnp.log(total)
        score_pos = jnp.sum(jnp.where(hit, score_blk, 0.0), axis=1, keepdims=True)
        loss_sum = loss_sum + jnp.sum(weight * (log_total - score_pos), axis=0, keepdims=True)
        grad_blk = weight * (exp_blk / total - jnp.where(hit, 1.0, 0.0))
        grad_pool = weight * (exp_pool / total)
        both = jnp.sum(grad_blk * raw_blk, axis=1, keepdims=True) + jnp.sum(grad_pool * raw_pool, axis=1, keepdims=True)
        scale_sum = scale_sum + INV_ROOT * jnp.sum(both, axis=0, keepdims=True)
        low[pl.ds(c * SLOTS, SLOTS), 0:TP] = grad_blk
        low[pl.ds(c * SLOTS, SLOTS), 256:256 + POOL] = grad_pool
        low_blk, low_pool = grad_blk.astype(BF16), grad_pool.astype(BF16)
        for b in range(4):
            cols = slice(b * W, (b + 1) * W)
            part = jnp.dot(low_blk, p_ref[:, cols], preferred_element_type=F32)
            part = part + jnp.dot(low_pool, pool[:, cols], preferred_element_type=F32)
            stack[b * SLOTS:(b + 1) * SLOTS, :] = (factor * part).astype(BF16)
        mixed = jnp.dot(mix, stack[...], preferred_element_type=F32).astype(BF16)
        gsnd[pl.ds(c * PER, PER)] = mixed.reshape(PER, 16, W)
        return loss_sum, scale_sum

    def bundles(ref, c):
        lo = 1 if c == 0 else c * PER
        return ref.at[pl.ds(lo, (c + 1) * PER - lo)]

    def owner_step(c, sums):
        some = bundles(rcv, c)
        copy(some, some, d_send, d_recv.at[c], here).wait_recv()
        some = bundles(mrcv, c)
        copy(some, some, m_send, m_recv.at[c], here).wait_recv()
        sums = work(c, sums)

        def back(o, carry):
            dz, dx = offset(o)
            copy(gsnd.at[o], grcv.at[o], g_send, g_recv.at[o // PER], cluster_peer(-dz, -dx)).start()
            return carry

        lax.fori_loop(1 if c == 0 else c * PER, (c + 1) * PER, back, 0)
        return sums

    sums = (jnp.zeros((1, 1), F32), jnp.zeros((1, 1), F32))
    for c in range(CHUNKS):
        sums = owner_step(c, sums)
    grcv[0] = gsnd[0]

    low[:, TP:256] = jnp.zeros((256, 256 - TP), F32)
    lowt[...] = low[...].T.astype(BF16)

    def pool_term(k, carry):
        cols = pl.ds(pl.multiple_of(k * 512, 512), 512)
        part = jnp.dot(lowt[256:256 + POOL, :], routed[:, cols], preferred_element_type=F32)
        pt[k % 2, k // 2] = factor * part
        return carry

    lax.fori_loop(0, 8, pool_term, 0)
    tile_lane = iota((8, 128), 1)
    sc[0] = jnp.where(tile_lane == 0, sums[0], jnp.where(tile_lane == 1, sums[1], 0.0))

    peer = group_peer(y, 1 - core)
    move = [
        copy(pt.at[1 - core], rc, r_send.at[0], r_recv.at[0], peer),
        copy(sc.at[0], rcs, t_send.at[0], t_recv.at[0], peer),
    ]
    for one in move:
        one.start()

    def passage_term(k, carry):
        cols = pl.ds(pl.multiple_of(k * 512, 512), 512)
        part = jnp.dot(lowt[0:TP, :], routed[:, cols], preferred_element_type=F32)
        pg_ref[:, cols] = (factor * part).astype(BF16)
        return carry

    lax.fori_loop(0, 8, passage_term, 0)
    for one in move:
        one.wait()
    s1[...] = pt[core] + rc[...]
    sc[1] = sc[0] + rcs[...]

    for k in range(1, NY):
        to = (y + k) % NY
        copy(s1.at[to], ry.at[k - 1], r_send.at[1], r_recv.at[1], group_peer(to, core)).start()
        copy(sc.at[1], rys.at[k - 1], t_send.at[1], t_recv.at[1], group_peer(to, core)).start()
    copy(ry, ry, r_send.at[1], r_recv.at[1], here).wait()
    copy(rys, rys, t_send.at[1], t_recv.at[1], here).wait()
    s2[...] = (s1[y] + ry[0] + ry[1] + ry[2]).reshape(NX, 32, 512)
    sc[2] = sc[1] + rys[0] + rys[1] + rys[2]

    for k in range(1, NX):
        to = (x + k) % NX
        copy(s2.at[to], rx.at[k - 1], r_send.at[2], r_recv.at[2], cluster_peer(0, k)).start()
        copy(sc.at[2], rxs.at[k - 1], t_send.at[2], t_recv.at[2], cluster_peer(0, k)).start()
    copy(rx, rx, r_send.at[2], r_recv.at[2], here).wait()
    copy(rxs, rxs, t_send.at[2], t_recv.at[2], here).wait()
    s3 = s2[x] + rx[0] + rx[1] + rx[2]
    scalars = sc[2] + rxs[0] + rxs[1] + rxs[2]
    for r in range(2):
        for cb in range(4):
            zb[:, r * 4 + cb, :] = s3[r * NZ:(r + 1) * NZ, cb * 128:(cb + 1) * 128]
    zb[:, 8:16, :] = jnp.broadcast_to(scalars[None], (NZ, 8, 128))

    def to_z(k, carry):
        copy(zb.at[(z + k) % NZ], rz.at[k - 1], r_send.at[3], r_recv.at[3], cluster_peer(k, 0)).start()
        return carry

    lax.fori_loop(1, NZ, to_z, 0)
    copy(rz, rz, r_send.at[3], r_recv.at[3], here).wait()
    last = zb[z] + jnp.sum(rz[...], axis=0)
    fin[...] = last[0:8]
    gb[grp] = last[0:8]
    loss_ref[0] = jnp.sum(jnp.where(tile_lane[0:1] == 0, last[8:9], 0.0)) * (1.0 / (TQ * OWNERS * 8))
    sgrad_ref[0] = jnp.sum(jnp.where(tile_lane[0:1] == 1, last[8:9], 0.0))

    def to_group(k, carry):
        copy(fin, gb.at[grp], r_send.at[4], r_recv.at[4], ((grp + k) % 8, clu)).start()
        return carry

    lax.fori_loop(1, 8, to_group, 0)

    def take(c):
        some = bundles(grcv, c)
        copy(some, some, g_send, g_recv.at[c], here).wait_recv()
        rows = grcv[pl.ds(c * PER, PER)].reshape(PER * 16, W)
        lanes = iota((TQ, PER * 16), 1) + c * (PER * 16)
        for b in range(4):
            part = jnp.dot(onehot(lanes == place_col + 4 * b), rows, preferred_element_type=F32)
            if c == 0:
                acc[:, b * W:(b + 1) * W] = part
            elif c + 1 < CHUNKS:
                acc[:, b * W:(b + 1) * W] += part
            else:
                home_ref[:, b * W:(b + 1) * W] = (acc[:, b * W:(b + 1) * W] + part).astype(BF16)

    for c in range(CHUNKS):
        take(c)

    some = gb.at[pl.ds(0, 7)]
    copy(some, some, r_send.at[4], r_recv.at[4], here).wait()
    for g in range(8):
        for r in range(2):
            for cb in range(4):
                col = g * 512 + cb * 128
                poolg_ref[r:r + 1, col:col + 128] = gb[g, r * 4 + cb:r * 4 + cb + 1, :]

    some = rcv.at[pl.ds(1, OWNERS - 1)]
    copy(some, some, d_send, d_recv.at[0], here).wait_send()
    copy(some, some, g_send, g_recv.at[0], here).wait_send()
    some = mrcv.at[pl.ds(1, OWNERS - 1)]
    copy(some, some, m_send, m_recv.at[0], here).wait_send()


def per_device(queries, cluster_id, block_list, positive, passages, pool_rows, logit_scale):
    piece = pool_rows.reshape(2, 4, 8, 128).transpose(1, 0, 2, 3).reshape(4, 16, 128)
    vm = pl.BlockSpec(memory_space=pltpu.VMEM)
    sm = pl.BlockSpec(memory_space=pltpu.SMEM)
    bundle = pltpu.VMEM((OWNERS, 16, W), BF16)
    note = pltpu.VMEM((OWNERS, 1, 128), F32)
    dma = pltpu.SemaphoreType.DMA
    home, passage_grad, pool_grad, loss, scale_grad = pl.pallas_call(
        kernel,
        out_shape=(
            jax.ShapeDtypeStruct((TQ, D), BF16),
            jax.ShapeDtypeStruct((TP, D), BF16),
            jax.ShapeDtypeStruct((2, D), F32),
            jax.ShapeDtypeStruct((1,), F32),
            jax.ShapeDtypeStruct((1,), F32),
        ),
        in_specs=[vm] * 6 + [sm],
        out_specs=(vm, vm, vm, sm, sm),
        scratch_shapes=[
            bundle, bundle, note, note, bundle, bundle,
            pltpu.VMEM((256, W), BF16),
            pltpu.VMEM((256, D), BF16),
            pltpu.VMEM((256, 384), F32),
            pltpu.VMEM((384, 256), BF16),
            pltpu.VMEM((TQ, D), F32),
            pltpu.VMEM((NY, NX, NZ, 16, 128), BF16),
            pltpu.VMEM((POOL, D), BF16),
            pltpu.VMEM((2, NY, POOL, 512), F32),
            pltpu.VMEM((NY, POOL, 512), F32),
            pltpu.VMEM((NY, POOL, 512), F32),
            pltpu.VMEM((NY - 1, POOL, 512), F32),
            pltpu.VMEM((NX, 32, 512), F32),
            pltpu.VMEM((NX - 1, 32, 512), F32),
            pltpu.VMEM((NZ, 16, 128), F32),
            pltpu.VMEM((NZ - 1, 16, 128), F32),
            pltpu.VMEM((8, 128), F32),
            pltpu.VMEM((8, 8, 128), F32),
            pltpu.VMEM((3, 8, 128), F32),
            pltpu.VMEM((8, 128), F32),
            pltpu.VMEM((NY - 1, 8, 128), F32),
            pltpu.VMEM((NX - 1, 8, 128), F32),
            dma, dma((CHUNKS,)), dma, dma((CHUNKS,)), dma, dma((CHUNKS,)),
            dma((3,)), dma((3,)), dma((5,)), dma((5,)), dma((3,)), dma((3,)),
        ],
        compiler_params=pltpu.CompilerParams(
            collective_id=0, has_side_effects=True, vmem_limit_bytes=48 * 1024 * 1024
        ),
        cost_estimate=pl.CostEstimate(flops=4 * 10**9, bytes_accessed=6 * 10**6, transcendentals=82000),
    )(
        queries,
        cluster_id.reshape(1, TQ),
        block_list.T,
        positive.reshape(1, TQ),
        passages,
        piece,
        logit_scale,
    )
    return home, passage_grad, pool_grad, loss, scale_grad


def solution(mesh):
    placed = (
        P(("group", "cluster"), None),
        P(("group", "cluster"), None),
        P(("group", "cluster"), None),
        P(("group", "cluster")),
        P(("group", "cluster"), None),
        P("cluster", None),
        P(),
    )
    return jax.shard_map(
        per_device,
        mesh=mesh,
        in_specs=placed,
        out_specs=(
            P(("group", "cluster"), None),
            P(("group", "cluster"), None),
            P("cluster", None),
            P(),
            P(),
        ),
        check_vma=False,
    )
```

time: 767 us -> 230 us (0.30)
  waiting for transfers between devices: 506 us -> 0 us
  Pallas kernels: 0 us -> 217 us
  blocking collectives: 162 us -> 0 us
  starting transfers between devices: 35.7 us -> 0 us
  matrix products: 20.2 us -> 0 us
  between operations: 17.9 us -> 4.8 us
  local copies, waits for them, and re-layouts: 20.3 us -> 7.98 us
    psum x1 -> x0, waiting for transfers between devices: 344 us -> none  [per_device(): summed = lax.psum(pool_term, ('group', 'cluster'))]
    pallas_call x0 -> x1, Pallas kernels: none -> 217 us  [per_device(): pl.pallas_call(kernel, out_shape=(jax.ShapeDtypeStruct((TQ, D), BF16), ja...]
    psum x1 -> x0, blocking collectives: 162 us -> none  [per_device(): lax.psum((loss_part, scale_part), ('group', 'cluster'))]
    all_gather x1 -> x0, waiting for transfers between devices: 153 us -> none  [per_device(): pool_all = lax.all_gather(pool_rows, 'cluster', axis=0, tiled=True)]
    all_to_all x3 -> x0, starting transfers between devices: 35.6 us -> none  [the longest x1 19.1 us: per_device(): lax.all_to_all(send_meta.reshape(owners, capacity, kcount + 2), 'cluster'...]
    dot_general x9 -> x0, matrix products: 20.2 us -> none  [the longest x1 3.43 us: per_device(): lax.dot_general(low_pool, routed, (((0,), (0,)), ((), ())), preferred_ele...]
    reshape x7 -> x1, local copies, waits for them, and re-layouts: 17.2 us -> 0.72 us  [per_device(): pool_rows.reshape(2, 4, 8, 128).transpose(1, 0, 2, 3).reshape(4, 16, 128)]
  transfers between devices with their start and end apart: 5 -> 0, of which waited for: 3 -> 0; matrix products, arithmetic and copies ran while one was open for 2% -> 0% of each run, Pallas kernels for 0% -> 0%
where the time goes in v1:
time: 230 us
  Pallas kernels  217 us (94%)
  local copies, waits for them, and re-layouts  7.98 us (3%)
  between operations  4.8 us (2%)
    pallas_call x1, Pallas kernels, per_device(): pl.pallas_call(kernel, out_shape=(jax.ShapeDtypeStruct((TQ, D), BF16), ja...  217 us
    unnamed x13, local copies, waits for them, and re-layouts  7.26 us

profile of v1, /device:TPU:1, one launch (start us, length us, event | category | flops | bytes accessed | tf_op | source)
XLA Modules:
  0.0 230.0 jit_solution(9555876914803820263)
XLA Ops:
  1.3 0.7 copy_bitcast_fusion.1.piece_ref
  2.0 0.0 copy-start
  2.0 1.4 copy-done
  3.4 0.0 copy-start.1
  3.4 1.2 copy-done.1
  4.6 0.0 copy-start.2
  4.6 0.7 copy-done.2
  5.3 0.0 copy-start.3
  5.3 0.7 copy-done.3
  5.9 0.0 copy-start.4
  5.9 0.7 copy-done.4
  6.6 217.2 %shard_map.110 = (bf16[112,4096]{1,0:T(8,128)(2,1)S(1)}, bf16[192,4096]{1,0:T(8,128)(2,1)S(1)}, f32[2,4096]{1,0:T(2,128)S(1)}, f32[1]{0:T(128)}, f32[1]{0:T(128)}) custom-call(bf16[112,4096]{1,0:T(8,128)(2,1)S(1)} %copy-done.1, s32[1,112]{1,0:T(1,128)S(1)} %bitcast.13, s32[2,112]{1,0:T(2,128)S(1)} %bitcast.12, s32[1,112]{1,0:T(1,128)S(1)} %bitcast.14, ...), custom_call_target="tpu_custom_call" | custom-call | flops 4000000000 | bytes 6000000 | tf_op jit(solution)/shard_map/pallas_call | solution.py:359
  223.8 0.9 copy.23
  224.7 1.1 copy.24
  225.8 0.6 copy.25
Async XLA Ops:
  2.0 1.4 copy-start
  3.4 1.2 copy-start.1
  4.6 0.7 copy-start.2
  5.3 0.7 copy-start.3
  5.9 0.7 copy-start.4

commit v2 on v1

--- a/solution.py
+++ b/solution.py
@@ -35,7 +35,7 @@
     return jnp.where(mask, 1.0, 0.0).astype(BF16)
 
 
-def kernel(
+def full_kernel(
     q_ref, cl_ref, bl_ref, pos_ref, p_ref, piece_ref, scale_ref,
     home_ref, pg_ref, poolg_ref, loss_ref, sgrad_ref,
     snd, rcv, msnd, mrcv, gsnd, grcv, stack, routed, low, lowt, acc, gp, pool,
@@ -349,15 +349,569 @@
     copy(some, some, m_send, m_recv.at[0], here).wait_send()
 
 
-def per_device(queries, cluster_id, block_list, positive, passages, pool_rows, logit_scale):
-    piece = pool_rows.reshape(2, 4, 8, 128).transpose(1, 0, 2, 3).reshape(4, 16, 128)
+BASE = 2
+V = D // 8
+SPARE = 12
+RING = 4 * SPARE
+LATE = 2 * NZ
+
+
+def fast_kernel(
+    q_ref, cl_ref, bl_ref, pos_ref, p_ref, piece_ref, scale_ref,
+    home_ref, pg_ref, poolg_ref, loss_ref, sgrad_ref, flag_ref,
+    snd, rcv, msnd, mrcv, gsnd, grcv, stack, routed, low, lowt, acc, gp, pool,
+    og, tg, px, pv, pts, ptr, rsn, rv, cc, rr, ll, late,
+    pt, rc, s1, ry, s2, rx, zb, rz, fin, gb, sc, rcs, rys, rxs,
+    d_send, d_recv, m_send, m_recv, g_send, g_recv, p_send, p_recv, r_send, r_recv, t_send, t_recv,
+    f_send, fr_recv, fl_recv, b_send, br_recv, bl_recv, x_send, x_recv,
+):
+    grp = lax.axis_index("group")
+    clu = lax.axis_index("cluster")
+    y, core = grp // 2, grp % 2
+    z, x = clu // NX, clu % NX
+
+    def cluster_peer(dz, dx):
+        return (grp, ((z + dz + NZ) % NZ) * NX + (x + dx + NX) % NX)
+
+    def group_peer(py, pc):
+        return (py * 2 + pc, clu)
+
+    def offset(o):
+        return ((o // 4) % 4) * 4 + o // 16, o % 4
+
+    def copy(src, dst, send, recv, peer):
+        return pltpu.make_async_remote_copy(
+            src_ref=src, dst_ref=dst, send_sem=send, recv_sem=recv, device_id=peer, device_id_type=MESH
+        )
+
+    here = (grp, clu)
+    barrier = pltpu.get_barrier_semaphore()
+
+    def greet(o, carry):
+        dz, dx = offset(o)
+        pl.semaphore_signal(barrier, inc=1, device_id=cluster_peer(dz, dx), device_id_type=MESH)
+        return carry
+
+    lax.fori_loop(1, OWNERS, greet, 0)
+
+    def greet_group(k, carry):
+        pl.semaphore_signal(barrier, inc=1, device_id=((grp + k) % 8, clu), device_id_type=MESH)
+        return carry
+
+    lax.fori_loop(1, 8, greet_group, 0)
+
+    factor = scale_ref[0] * INV_ROOT
+
+    a_iota, b_iota = iota((TQ, TQ), 0), iota((TQ, TQ), 1)
+    eye = a_iota == b_iota
+
+    def to_col(row):
+        return jnp.sum(jnp.where(eye, row.astype(F32), 0.0), axis=1, keepdims=True)
+
+    cl_row = cl_ref[...]
+    cl_col = to_col(cl_row).astype(jnp.int32)
+    same = cl_col == cl_row
+    rank_row = jnp.sum(jnp.where(same & (a_iota < b_iota), 1.0, 0.0), axis=0, keepdims=True).astype(jnp.int32)
+    rank_col = jnp.sum(jnp.where(same & (b_iota < a_iota), 1.0, 0.0), axis=1, keepdims=True).astype(jnp.int32)
+    extra_row, extra_col = rank_row >= BASE, rank_col >= BASE
+    spare_row = jnp.sum(jnp.where(extra_col & (a_iota < b_iota), 1.0, 0.0), axis=0, keepdims=True).astype(jnp.int32)
+    spare_col = jnp.sum(jnp.where(extra_row & (b_iota < a_iota), 1.0, 0.0), axis=1, keepdims=True).astype(jnp.int32)
+    fits_row, fits_col = extra_row & (spare_row < SPARE), extra_col & (spare_col < SPARE)
+    spare_row = jnp.where(fits_row, spare_row, -4096)
+    spare_col = jnp.where(fits_col, spare_col, -4096)
+    left_over = jnp.sum(jnp.where(extra_col & jnp.logical_not(fits_col), 1.0, 0.0), axis=0, keepdims=True)
+
+    def offset_of(cl):
+        dz = ((cl >> 2) - z) & 15
+        return (dz & 3) * 16 + (dz >> 2) * 4 + ((cl - x) & 3)
+
+    off_row, off_col = offset_of(cl_row), offset_of(cl_col)
+    place_row = jnp.where(extra_row, -4096, off_row * 16 + rank_row)
+    place_col = jnp.where(extra_col, -4096, off_col * 16 + rank_col)
+
+    lane = iota((TQ, 128), 1)
+    field = lane >> 2
+    block0, block1, position = to_col(bl_ref[0:1, :]), to_col(bl_ref[1:2, :]), to_col(pos_ref[...])
+    value = jnp.where(field == 0, block0, jnp.where(field == 1, block1, jnp.where(field == 2, position, 1.0)))
+    value = jnp.where((rank_col == (lane & 3)) & (field < 4) & jnp.logical_not(extra_col), value, 0.0).astype(BF16)
+    meta = jnp.dot(onehot(iota((OWNERS, TQ), 0) == off_row), value, preferred_element_type=F32)
+    msnd[:, 0, :] = meta
+
+    total = jnp.zeros((RING, W), F32)
+    for b in range(4):
+        pick = onehot(iota((RING, TQ), 0) == spare_row + SPARE * b)
+        total = total + jnp.dot(pick, q_ref[:, b * W:(b + 1) * W], preferred_element_type=F32)
+    og[z] = total.astype(BF16)
+    kind = iota((8, TQ), 0)
+    facts = jnp.where(
+        kind == 0, cl_row.astype(F32),
+        jnp.where(
+            kind == 1, bl_ref[0:1, :].astype(F32),
+            jnp.where(kind == 2, bl_ref[1:2, :].astype(F32), jnp.where(kind == 3, pos_ref[...].astype(F32), 1.0)),
+        ),
+    )
+    facts = jnp.where(kind < 5, facts, 0.0).astype(BF16)
+    spot = lane % SPARE
+    tg[z] = jnp.dot(facts, onehot((spot == spare_col) & (lane < RING)), preferred_element_type=F32)
+
+    def build(c):
+        row = iota((PER * 16, TQ), 0) + c * (PER * 16)
+        total = jnp.zeros((PER * 16, V), F32)
+        for b in range(8):
+            pick = onehot(row == place_row + BASE * b)
+            total = total + jnp.dot(pick, q_ref[:, b * V:(b + 1) * V], preferred_element_type=F32)
+        snd[pl.ds(c * PER, PER)] = total.astype(BF16).reshape(PER, 16, V)
+
+    def send_chunk(c):
+        def step(o, carry):
+            dz, dx = offset(o)
+            peer = cluster_peer(dz, dx)
+            copy(msnd.at[o], mrcv.at[o], m_send, m_recv.at[o // PER], peer).start()
+            copy(snd.at[o], rcv.at[o], d_send, d_recv.at[o // PER], peer).start()
+            return carry
+
+        lax.fori_loop(1 if c == 0 else c * PER, (c + 1) * PER, step, 0)
+
+    def right(k):
+        one = og.at[(z - k + 1 + NZ) % NZ]
+        return copy(one, one, f_send.at[0], fr_recv.at[k - 1], cluster_peer(1, 0))
+
+    def left(k):
+        one = og.at[(z + k - 1) % NZ]
+        return copy(one, one, f_send.at[1], fl_recv.at[k - 1], cluster_peer(-1, 0))
+
+    def ring(k):
+        if k > 1:
+            one = og.at[(z - k + 1 + NZ) % NZ]
+            copy(one, one, f_send.at[0], fr_recv.at[k - 2], here).wait_recv()
+            one = og.at[(z + k - 1) % NZ]
+            copy(one, one, f_send.at[1], fl_recv.at[k - 2], here).wait_recv()
+        right(k).start()
+        if k < 8:
+            left(k).start()
+
+    gp[y, x, z] = piece_ref[y]
+    pl.semaphore_wait(barrier, OWNERS - 1 + 7)
+    ring(1)
+
+    def early(k, carry):
+        copy(tg.at[z], tg.at[z], t_send.at[3], t_recv.at[3], cluster_peer(k, 0)).start()
+        copy(gp.at[y, x, z], gp.at[y, x, z], p_send.at[0], p_recv.at[0], cluster_peer(k, 0)).start()
+        return carry
+
+    lax.fori_loop(1, NZ, early, 0)
+    build(0)
+    send_chunk(0)
+    build(1)
+    ring(2)
+    some = gp.at[y, x, pl.ds(0, NZ - 1)]
+    copy(some, some, p_send.at[0], p_recv.at[0], here).wait()
+    for k in range(1, NX):
+        copy(gp.at[y, x], gp.at[y, x], p_send.at[1], p_recv.at[1], cluster_peer(0, k)).start()
+    ring(3)
+    send_chunk(1)
+    build(2)
+    ring(4)
+    some = gp.at[y, pl.ds(0, NX - 1)]
+    copy(some, some, p_send.at[1], p_recv.at[1], here).wait()
+    for k in range(1, NY):
+        copy(gp.at[y], gp.at[y], p_send.at[2], p_recv.at[2], group_peer((y + k) % NY, core)).start()
+    ring(5)
+    send_chunk(2)
+    build(3)
+    ring(6)
+    rcv[0] = snd[0]
+    mrcv[0] = msnd[0]
+    some = gp.at[pl.ds(0, NY - 1)]
+    copy(some, some, p_send.at[2], p_recv.at[2], here).wait()
+
+    def spread(yy, carry):
+        flat = gp[yy].reshape(OWNERS * 16, 128)
+        i, j = iota((POOL, OWNERS * 16), 0), iota((POOL, OWNERS * 16), 1)
+        base = (i >> 5) * (NZ * 16) + (i & 15) * 16 + ((i >> 4) & 1) * 8
+        for cb in range(8):
+            part = jnp.dot(onehot(j == base + cb), flat, preferred_element_type=F32).astype(BF16)
+            pool[:, pl.ds(pl.multiple_of(yy * W + cb * 128, 128), 128)] = part
+        return carry
+
+    some = tg.at[pl.ds(0, NZ - 1)]
+    copy(some, some, t_send.at[3], t_recv.at[3], here).wait()
+
+    ring(7)
+    send_chunk(3)
+    lax.fori_loop(0, NY, spread, 0)
+
+    def gather_facts(k, carry):
+        shift = onehot((iota((128, NZ * RING), 1) == iota((128, NZ * RING), 0) + k * RING) & (iota((128, NZ * RING), 0) < RING))
+        return carry + jnp.dot(tg[k].astype(BF16), shift, preferred_element_type=F32)
+
+    span = NZ * RING
+    known = lax.fori_loop(0, NZ, gather_facts, jnp.zeros((8, span), F32))
+    dest = known[0:1].astype(jnp.int32)
+    local = (known[4:5] > 0.5) & ((dest >> 2) == z)
+    across = iota((1, span), 1)
+    block_of = (across % RING) // SPARE
+    to_x = dest & 3
+    mark = (iota((8, span), 0) == to_x) & local & (block_of == 0)
+    before = onehot(iota((span, span), 0) < across - block_of * SPARE)
+    ranks = jnp.dot(onehot(mark), before, preferred_element_type=F32)
+    order = jnp.sum(jnp.where(iota((8, span), 0) == to_x, ranks, 0.0), axis=0, keepdims=True).astype(jnp.int32)
+    key = jnp.where(local, to_x * (4 * LATE) + block_of * LATE + order, -1)
+    first_key = jnp.where(local & (block_of == 0), to_x * LATE + order, -1)
+    key_col = jnp.broadcast_to(key.astype(F32), (8, span)).T[:, 0:1].astype(jnp.int32)
+    pts[...] = lax.dot_general(
+        known.astype(BF16), onehot(iota((NX * LATE, span), 0) == first_key), (((1,), (1,)), ((), ())),
+        preferred_element_type=F32,
+    )
+    ring(8)
+    one = og.at[(z + 8) % NZ]
+    copy(one, one, f_send.at[0], fr_recv.at[7], here).wait_recv()
+    for to in range(NX):
+        pick = onehot(iota((4 * LATE, span), 0) + to * (4 * LATE) == key)
+        px[to] = jnp.dot(pick, og[...].reshape(span, W), preferred_element_type=F32).astype(BF16)
+    for k in range(1, NX):
+        copy(px.at[(x + k) % NX], pv.at[x], x_send.at[0], x_recv.at[0], cluster_peer(0, k)).start()
+        copy(pts, ptr.at[x], x_send.at[1], x_recv.at[1], cluster_peer(0, k)).start()
+    pv[x] = px[x]
+    ptr[x] = pts[...]
+
+    i, j = iota((256, 256), 0), iota((256, 256), 1)
+    unmix = onehot(((i >> 1) & 15) * 16 + (i >> 5) * 2 + (i & 1) == j)
+    mix = onehot(((j >> 1) & 15) * 16 + (j >> 5) * 2 + (j & 1) == i)
+    contract = (((1,), (1,)), ((), ()))
+
+    def work(lo, count, columns, sums):
+        loss_sum, scale_sum = sums
+        first, second, place, weight = columns
+        mine = routed[lo:lo + count, :]
+        raw_blk = lax.dot_general(mine, p_ref[...], contract, preferred_element_type=F32)
+        raw_pool = lax.dot_general(mine, pool[...], contract, preferred_element_type=F32)
+        cand = iota((count, TP), 1)
+        block = (cand >> 6).astype(F32)
+        allowed = (block == first) | (block == second)
+        hit = cand.astype(F32) == first * BLOCK + place
+        score_blk = factor * raw_blk
+        score_pool = factor * raw_pool
+        peak = jnp.maximum(
+            jnp.max(jnp.where(allowed, score_blk, -jnp.inf), axis=1, keepdims=True),
+            jnp.max(score_pool, axis=1, keepdims=True),
+        )
+        exp_blk = jnp.where(allowed, jnp.exp(jnp.where(allowed, score_blk - peak, 0.0)), 0.0)
+        exp_pool = jnp.exp(score_pool - peak)
+        total = jnp.sum(exp_blk, axis=1, keepdims=True) + jnp.sum(exp_pool, axis=1, keepdims=True)
+        log_total = peak + jnp.log(total)
+        score_pos = jnp.sum(jnp.where(hit, score_blk, 0.0), axis=1, keepdims=True)
+        loss_sum = loss_sum + jnp.sum(weight * (log_total - score_pos), axis=0, keepdims=True)
+        grad_blk = weight * (exp_blk / total - jnp.where(hit, 1.0, 0.0))
+        grad_pool = weight * (exp_pool / total)
+        both = jnp.sum(grad_blk * raw_blk, axis=1, keepdims=True) + jnp.sum(grad_pool * raw_pool, axis=1, keepdims=True)
+        scale_sum = scale_sum + INV_ROOT * jnp.sum(both, axis=0, keepdims=True)
+        low[lo:lo + count, 0:TP] = grad_blk
+        low[lo:lo + count, 256:256 + POOL] = grad_pool
+        low_blk, low_pool = grad_blk.astype(BF16), grad_pool.astype(BF16)
+
+        def grads(cols):
+            part = jnp.dot(low_blk, p_ref[:, cols], preferred_element_type=F32)
+            part = part + jnp.dot(low_pool, pool[:, cols], preferred_element_type=F32)
+            return (factor * part).astype(BF16)
+
+        return (loss_sum, scale_sum), grads
+
+    def bundles(ref, c):
+        lo = 1 if c == 0 else c * PER
+        return ref.at[pl.ds(lo, (c + 1) * PER - lo)]
+
+    HALF = 2 * PER * BASE
+
+    def half(h, sums):
+        for c in (2 * h, 2 * h + 1):
+            some = bundles(rcv, c)
+            copy(some, some, d_send, d_recv.at[c], here).wait_recv()
+            some = bundles(mrcv, c)
+            copy(some, some, m_send, m_recv.at[c], here).wait_recv()
+            rows = rcv[pl.ds(c * PER, PER)].reshape(PER * 16, V)
+            plain = jnp.dot(unmix, rows, preferred_element_type=F32).astype(BF16)
+            for b in range(8):
+                routed[c * 32:(c + 1) * 32, b * V:(b + 1) * V] = plain[b * 32:(b + 1) * 32]
+        expand = onehot((iota((HALF, 2 * PER), 0) >> 1) == iota((HALF, 2 * PER), 1))
+        got = mrcv[pl.ds(2 * h * PER, 2 * PER), 0, :].astype(BF16)
+        got = jnp.dot(expand, got, preferred_element_type=F32)
+        lanes, rank = iota((HALF, 128), 1), iota((HALF, 128), 0) & 1
+
+        def column(f):
+            return jnp.sum(jnp.where(lanes == 4 * f + rank, got, 0.0), axis=1, keepdims=True)
+
+        sums, grads = work(h * HALF, HALF, [column(f) for f in range(4)], sums)
+        for b in range(8):
+            part = grads(slice(b * V, (b + 1) * V))
+            stack[0, b * 32:(b + 1) * 32, :] = part[0:32]
+            stack[1, b * 32:(b + 1) * 32, :] = part[32:64]
+        for c in (0, 1):
+            mixed = jnp.dot(mix, stack[c], preferred_element_type=F32).astype(BF16)
+            gsnd[pl.ds((2 * h + c) * PER, PER)] = mixed.reshape(PER, 16, V)
+        return sums
+
+    def send_back(c):
+        def back(o, carry):
+            dz, dx = offset(o)
+            copy(gsnd.at[o], grcv.at[o], g_send, g_recv.at[o // PER], cluster_peer(-dz, -dx)).start()
+            return carry
+
+        lax.fori_loop(1 if c == 0 else c * PER, (c + 1) * PER, back, 0)
+
+    sums = (jnp.zeros((1, 1), F32), jnp.zeros((1, 1), F32))
+    sums = half(0, sums)
+    send_back(0)
+    send_back(1)
+    grcv[0] = gsnd[0]
+
+    some = pv.at[pl.ds(0, NX - 1)]
+    copy(some, some, x_send.at[0], x_recv.at[0], here).wait()
+    some = ptr.at[pl.ds(0, NX - 1)]
+    copy(some, some, x_send.at[1], x_recv.at[1], here).wait()
+    choose = onehot(iota((LATE, 128), 1) == iota((LATE, 128), 0) + x * LATE)
+    for via in range(NX):
+        for b in range(4):
+            routed[128 + via * LATE:128 + (via + 1) * LATE, b * W:(b + 1) * W] = pv[via, b * LATE:(b + 1) * LATE, :]
+        late[via * LATE:(via + 1) * LATE, 0:8] = lax.dot_general(
+            choose, ptr[via].astype(BF16), contract, preferred_element_type=F32
+        )
+    sums, grads = work(128, 128, [late[:, f:f + 1] for f in range(1, 5)], sums)
+    for b in range(4):
+        part = grads(slice(b * W, (b + 1) * W))
+        for via in range(NX):
+            rsn[via, b * LATE:(b + 1) * LATE, :] = part[via * LATE:(via + 1) * LATE]
+    for k in range(1, NX):
+        copy(rsn.at[(x + k) % NX], rv.at[x], x_send.at[2], x_recv.at[2], cluster_peer(0, k)).start()
+    rv[x] = rsn[x]
+    sums = half(1, sums)
+
+    some = rv.at[pl.ds(0, NX - 1)]
+    copy(some, some, x_send.at[2], x_recv.at[2], here).wait()
+    cols_iota = iota((RING, NX * 4 * LATE), 1)
+    for k in range(NZ):
+        pick = onehot(cols_iota == key_col[k * RING:(k + 1) * RING])
+        cc[k] = jnp.dot(pick, rv[...].reshape(NX * 4 * LATE, W), preferred_element_type=F32).astype(BF16)
+
+    def ring_back(k):
+        to = (z + 9 - k) % NZ
+        if k > 1:
+            copy(rr.at[k - 2], rr.at[k - 2], b_send.at[0], br_recv.at[k - 2], here).wait_recv()
+            cc[to] = cc[to] + rr[k - 2]
+        copy(cc.at[to], rr.at[k - 1], b_send.at[0], br_recv.at[k - 1], cluster_peer(1, 0)).start()
+        if k < 8:
+            to = (z - 8 + k + NZ) % NZ
+            if k > 1:
+                copy(ll.at[k - 2], ll.at[k - 2], b_send.at[1], bl_recv.at[k - 2], here).wait_recv()
+                cc[to] = cc[to] + ll[k - 2]
+            copy(cc.at[to], ll.at[k - 1], b_send.at[1], bl_recv.at[k - 1], cluster_peer(-1, 0)).start()
+
+    ring_back(1)
+    send_back(2)
+
+    low[:, TP:256] = jnp.zeros((256, 256 - TP), F32)
+    lowt[...] = low[...].T.astype(BF16)
+
+    def pool_term(k, carry):
+        cols = pl.ds(pl.multiple_of(k * 512, 512), 512)
+        part = jnp.dot(lowt[256:256 + POOL, :], routed[:, cols], preferred_element_type=F32)
+        pt[k % 2, k // 2] = factor * part
+        return carry
+
+    lax.fori_loop(0, 8, pool_term, 0)
+    tile_lane = iota((8, 128), 1)
+    sc[0] = jnp.where(
+        tile_lane == 0, sums[0], jnp.where(tile_lane == 1, sums[1], jnp.where(tile_lane == 2, left_over, 0.0))
+    )
+
+    peer = group_peer(y, 1 - core)
+    move = [
+        copy(pt.at[1 - core], rc, r_send.at[0], r_recv.at[0], peer),
+        copy(sc.at[0], rcs, t_send.at[0], t_recv.at[0], peer),
+    ]
+    for one in move:
+        one.start()
+    ring_back(2)
+    send_back(3)
+
+    def passage_term(k, carry):
+        cols = pl.ds(pl.multiple_of(k * 512, 512), 512)
+        part = jnp.dot(lowt[0:TP, :], routed[:, cols], preferred_element_type=F32)
+        pg_ref[:, cols] = (factor * part).astype(BF16)
+        return carry
+
+    lax.fori_loop(0, 8, passage_term, 0)
+    for one in move:
+        one.wait()
+    s1[...] = pt[core] + rc[...]
+    sc[1] = sc[0] + rcs[...]
+
+    for k in range(1, NY):
+        to = (y + k) % NY
+        copy(s1.at[to], ry.at[k - 1], r_send.at[1], r_recv.at[1], group_peer(to, core)).start()
+        copy(sc.at[1], rys.at[k - 1], t_send.at[1], t_recv.at[1], group_peer(to, core)).start()
+    ring_back(3)
+    copy(ry, ry, r_send.at[1], r_recv.at[1], here).wait()
+    copy(rys, rys, t_send.at[1], t_recv.at[1], here).wait()
+    s2[...] = (s1[y] + ry[0] + ry[1] + ry[2]).reshape(NX, 32, 512)
+    sc[2] = sc[1] + rys[0] + rys[1] + rys[2]
+
+    for k in range(1, NX):
+        to = (x + k) % NX
+        copy(s2.at[to], rx.at[k - 1], r_send.at[2], r_recv.at[2], cluster_peer(0, k)).start()
+        copy(sc.at[2], rxs.at[k - 1], t_send.at[2], t_recv.at[2], cluster_peer(0, k)).start()
+    ring_back(4)
+    copy(rx, rx, r_send.at[2], r_recv.at[2], here).wait()
+    copy(rxs, rxs, t_send.at[2], t_recv.at[2], here).wait()
+    s3 = s2[x] + rx[0] + rx[1] + rx[2]
+    scalars = sc[2] + rxs[0] + rxs[1] + rxs[2]
+    for r in range(2):
+        for cb in range(4):
+            zb[:, r * 4 + cb, :] = s3[r * NZ:(r + 1) * NZ, cb * 128:(cb + 1) * 128]
+    zb[:, 8:16, :] = jnp.broadcast_to(scalars[None], (NZ, 8, 128))
+
+    def to_z(k, carry):
+        copy(zb.at[(z + k) % NZ], rz.at[k - 1], r_send.at[3], r_recv.at[3], cluster_peer(k, 0)).start()
+        return carry
+
+    lax.fori_loop(1, NZ, to_z, 0)
+    ring_back(5)
+    ring_back(6)
+    copy(rz, rz, r_send.at[3], r_recv.at[3], here).wait()
+    last = zb[z] + jnp.sum(rz[...], axis=0)
+    fin[...] = last[0:8]
+    gb[grp] = last[0:8]
+    loss_ref[0] = jnp.sum(jnp.where(tile_lane[0:1] == 0, last[8:9], 0.0)) * (1.0 / (TQ * OWNERS * 8))
+    sgrad_ref[0] = jnp.sum(jnp.where(tile_lane[0:1] == 1, last[8:9], 0.0))
+    flag_ref[0] = jnp.sum(jnp.where(tile_lane[0:1] == 2, last[8:9], 0.0))
+
+    def to_group(k, carry):
+        copy(fin, gb.at[grp], r_send.at[4], r_recv.at[4], ((grp + k) % 8, clu)).start()
+        return carry
+
+    lax.fori_loop(1, 8, to_group, 0)
+    ring_back(7)
+
+    def take(c):
+        some = bundles(grcv, c)
+        copy(some, some, g_send, g_recv.at[c], here).wait_recv()
+        rows = grcv[pl.ds(c * PER, PER)].reshape(PER * 16, V)
+        lanes = iota((TQ, PER * 16), 1) + c * (PER * 16)
+        for b in range(8):
+            part = jnp.dot(onehot(lanes == place_col + BASE * b), rows, preferred_element_type=F32)
+            if c == 0:
+                acc[:, b * V:(b + 1) * V] = part
+            else:
+                acc[:, b * V:(b + 1) * V] += part
+
+    take(0)
+    ring_back(8)
+    for c in range(1, CHUNKS):
+        take(c)
+    copy(rr.at[7], rr.at[7], b_send.at[0], br_recv.at[7], here).wait_recv()
+    copy(ll.at[6], ll.at[6], b_send.at[1], bl_recv.at[6], here).wait_recv()
+    spare_rows = cc[z] + rr[7] + ll[6]
+    for b in range(4):
+        pick = onehot(iota((TQ, RING), 1) == spare_col + SPARE * b)
+        part = jnp.dot(pick, spare_rows, preferred_element_type=F32)
+        home_ref[:, b * W:(b + 1) * W] = (acc[:, b * W:(b + 1) * W] + part).astype(BF16)
+
+    some = gb.at[pl.ds(0, 7)]
+    copy(some, some, r_send.at[4], r_recv.at[4], here).wait()
+    for g in range(8):
+        for r in range(2):
+            for cb in range(4):
+                col = g * 512 + cb * 128
+                poolg_ref[r:r + 1, col:col + 128] = gb[g, r * 4 + cb:r * 4 + cb + 1, :]
+
+    some = rcv.at[pl.ds(1, OWNERS - 1)]
+    copy(some, some, d_send, d_recv.at[0], here).wait_send()
+    copy(some, some, g_send, g_recv.at[0], here).wait_send()
+    some = mrcv.at[pl.ds(1, OWNERS - 1)]
+    copy(some, some, m_send, m_recv.at[0], here).wait_send()
+    for side, count in ((0, 8), (1, 7)):
+        some = og.at[pl.ds(0, count)]
+        copy(some, some, f_send.at[side], fr_recv.at[0], here).wait_send()
+        some = cc.at[pl.ds(0, count)]
+        copy(some, some, b_send.at[side], br_recv.at[0], here).wait_send()
+
+
+def reduce_scratch():
+    return [
+        pltpu.VMEM((2, NY, POOL, 512), F32),
+        pltpu.VMEM((NY, POOL, 512), F32),
+        pltpu.VMEM((NY, POOL, 512), F32),
+        pltpu.VMEM((NY - 1, POOL, 512), F32),
+        pltpu.VMEM((NX, 32, 512), F32),
+        pltpu.VMEM((NX - 1, 32, 512), F32),
+        pltpu.VMEM((NZ, 16, 128), F32),
+        pltpu.VMEM((NZ - 1, 16, 128), F32),
+        pltpu.VMEM((8, 128), F32),
+        pltpu.VMEM((8, 8, 128), F32),
+        pltpu.VMEM((3, 8, 128), F32),
+        pltpu.VMEM((8, 128), F32),
+        pltpu.VMEM((NY - 1, 8, 128), F32),
+        pltpu.VMEM((NX - 1, 8, 128), F32),
+    ]
+
+
+def fast_call(*args):
+    vm = pl.BlockSpec(memory_space=pltpu.VMEM)
+    sm = pl.BlockSpec(memory_space=pltpu.SMEM)
+    bundle = pltpu.VMEM((OWNERS, 16, V), BF16)
+    note = pltpu.VMEM((OWNERS, 1, 128), F32)
+    column = pltpu.VMEM((NX, 4 * LATE, W), BF16)
+    dma = pltpu.SemaphoreType.DMA
+    scalar = jax.ShapeDtypeStruct((1,), F32)
+    return pl.pallas_call(
+        fast_kernel,
+        out_shape=(
+            jax.ShapeDtypeStruct((TQ, D), BF16),
+            jax.ShapeDtypeStruct((TP, D), BF16),
+            jax.ShapeDtypeStruct((2, D), F32),
+            scalar, scalar, scalar,
+        ),
+        in_specs=[vm] * 6 + [sm],
+        out_specs=(vm, vm, vm, sm, sm, sm),
+        scratch_shapes=[
+            bundle, bundle, note, note, bundle, bundle,
+            pltpu.VMEM((2, 256, V), BF16),
+            pltpu.VMEM((256, D), BF16),
+            pltpu.VMEM((256, 384), F32),
+            pltpu.VMEM((384, 256), BF16),
+            pltpu.VMEM((TQ, D), F32),
+            pltpu.VMEM((NY, NX, NZ, 16, 128), BF16),
+            pltpu.VMEM((POOL, D), BF16),
+            pltpu.VMEM((NZ, RING, W), BF16),
+            pltpu.VMEM((NZ, 8, 128), F32),
+            column, column,
+            pltpu.VMEM((8, 128), F32),
+            pltpu.VMEM((NX, 8, 128), F32),
+            column, column,
+            pltpu.VMEM((NZ, RING, W), BF16),
+            pltpu.VMEM((8, RING, W), BF16),
+            pltpu.VMEM((7, RING, W), BF16),
+            pltpu.VMEM((128, 128), F32),
+            *reduce_scratch(),
+            dma, dma((CHUNKS,)), dma, dma((CHUNKS,)), dma, dma((CHUNKS,)),
+            dma((3,)), dma((3,)), dma((5,)), dma((5,)), dma((4,)), dma((4,)),
+            dma((2,)), dma((8,)), dma((7,)), dma((2,)), dma((8,)), dma((7,)), dma((3,)), dma((3,)),
+        ],
+        compiler_params=pltpu.CompilerParams(
+            collective_id=1, has_side_effects=True, vmem_limit_bytes=48 * 1024 * 1024
+        ),
+        cost_estimate=pl.CostEstimate(flops=4 * 10**9, bytes_accessed=6 * 10**6, transcendentals=82000),
+    )(*args)
+
+
+def full_call(*args):
     vm = pl.BlockSpec(memory_space=pltpu.VMEM)
     sm = pl.BlockSpec(memory_space=pltpu.SMEM)
     bundle = pltpu.VMEM((OWNERS, 16, W), BF16)
     note = pltpu.VMEM((OWNERS, 1, 128), F32)
     dma = pltpu.SemaphoreType.DMA
-    home, passage_grad, pool_grad, loss, scale_grad = pl.pallas_call(
-        kernel,
+    return pl.pallas_call(
+        full_kernel,
         out_shape=(
             jax.ShapeDtypeStruct((TQ, D), BF16),
             jax.ShapeDtypeStruct((TP, D), BF16),
@@ -376,20 +930,7 @@
             pltpu.VMEM((TQ, D), F32),
             pltpu.VMEM((NY, NX, NZ, 16, 128), BF16),
             pltpu.VMEM((POOL, D), BF16),
-            pltpu.VMEM((2, NY, POOL, 512), F32),
-            pltpu.VMEM((NY, POOL, 512), F32),
-            pltpu.VMEM((NY, POOL, 512), F32),
-            pltpu.VMEM((NY - 1, POOL, 512), F32),
-            pltpu.VMEM((NX, 32, 512), F32),
-            pltpu.VMEM((NX - 1, 32, 512), F32),
-            pltpu.VMEM((NZ, 16, 128), F32),
-            pltpu.VMEM((NZ - 1, 16, 128), F32),
-            pltpu.VMEM((8, 128), F32),
-            pltpu.VMEM((8, 8, 128), F32),
-            pltpu.VMEM((3, 8, 128), F32),
-            pltpu.VMEM((8, 128), F32),
-            pltpu.VMEM((NY - 1, 8, 128), F32),
-            pltpu.VMEM((NX - 1, 8, 128), F32),
+            *reduce_scratch(),
             dma, dma((CHUNKS,)), dma, dma((CHUNKS,)), dma, dma((CHUNKS,)),
             dma((3,)), dma((3,)), dma((5,)), dma((5,)), dma((3,)), dma((3,)),
         ],
@@ -397,7 +938,12 @@
             collective_id=0, has_side_effects=True, vmem_limit_bytes=48 * 1024 * 1024
         ),
         cost_estimate=pl.CostEstimate(flops=4 * 10**9, bytes_accessed=6 * 10**6, transcendentals=82000),
-    )(
+    )(*args)
+
+
+def per_device(queries, cluster_id, block_list, positive, passages, pool_rows, logit_scale):
+    piece = pool_rows.reshape(2, 4, 8, 128).transpose(1, 0, 2, 3).reshape(4, 16, 128)
+    args = (
         queries,
         cluster_id.reshape(1, TQ),
         block_list.T,
@@ -406,7 +952,8 @@
         piece,
         logit_scale,
     )
-    return home, passage_grad, pool_grad, loss, scale_grad
+    *quick, left_over = fast_call(*args)
+    return lax.cond(left_over[0] > 0.5, lambda: tuple(full_call(*args)), lambda: tuple(quick))
 
 
 def solution(mesh):

time: 230 us -> 206 us (0.90); the launches traced: 230 us -> 203 us
  Pallas kernels: 217 us -> 194 us
  local copies, waits for them, and re-layouts: 7.98 us -> 3.42 us
    pallas_call x1, Pallas kernels: 217 us -> 194 us  [fast_call(): pl.pallas_call(fast_kernel, out_shape=(jax.ShapeDtypeStruct((TQ, D), BF16...]
    unnamed x13 -> x11, local copies, waits for them, and re-layouts: 7.26 us -> 2.7 us
where the time goes in v2:
time: 206 us; the launch traced here: 203 us
  Pallas kernels  194 us (94%)
  between operations  5.47 us (3%)
  local copies, waits for them, and re-layouts  3.42 us (2%)
    pallas_call x1, Pallas kernels, fast_call(): pl.pallas_call(fast_kernel, out_shape=(jax.ShapeDtypeStruct((TQ, D), BF16...  194 us

profile of v2, /device:TPU:1, one launch (start us, length us, event | category | flops | bytes accessed | tf_op | source)
XLA Modules:
  0.0 203.1 jit_solution(9007412291078701730)
XLA Ops:
  1.3 0.7 copy_bitcast_fusion.1.piece_ref
  2.0 0.0 copy-start
  2.0 0.0 copy-start.1
  2.0 0.0 copy-start.2
  2.0 0.0 copy-start.3
  2.0 194.2 %shard_map.120 = (bf16[112,4096]{1,0:T(8,128)(2,1)S(1)}, bf16[192,4096]{1,0:T(8,128)(2,1)S(1)}, f32[2,4096]{1,0:T(2,128)S(1)}, f32[1]{0:T(128)}, f32[1]{0:T(128)}, /*index=5*/f32[1]{0:T(128)}) custom-call(bf16[112,4096]{1,0:T(8,128)(2,1)} %q_ref.1, s32[1,112]{1,0:T(1,128)} %bitcast.16, s32[2,112]{1,0:T(2,128)} %bitcast.14, s32[1,112]{1,0:T(1,128)} %bitcast.18, ...), custom_call_target="tpu_custom_call" | custom-call | flops 4000000000 | bytes 6000000 | tf_op jit(solution)/shard_map/pallas_call | solution.py:866
  196.8 0.0 copy-done
  196.8 0.0 copy-done.1
  196.8 0.0 copy-done.2
  196.8 0.0 copy-done.3
  196.9 0.9 copy.43
  197.8 1.1 copy.44
  198.9 0.6 copy.45
  (1 shorter events, 0.0 us)
Async XLA Ops:
  2.0 194.8 %copy-start = (bf16[112,4096]{1,0:T(8,128)(2,1)S(1)}, bf16[112,4096]{1,0:T(8,128)(2,1)}, u32[]{:S(2)}) copy-start(bf16[112,4096]{1,0:T(8,128)(2,1)} %q_ref.1) | copy-start | bytes 2752516
  2.0 194.8 %copy-start.1 = (s32[112,2]{0,1:T(2,128)S(1)}, s32[112,2]{0,1:T(2,128)}, u32[]{:S(2)}) copy-start(s32[112,2]{0,1:T(2,128)} %param.11) | copy-start | bytes 2692
  2.0 194.8 %copy-start.2 = (s32[112,1]{0,1:T(1,128)S(1)}, s32[112,1]{0,1:T(1,128)}, u32[]{:S(2)}) copy-start(s32[112,1]{0,1:T(1,128)} %param.10) | copy-start | bytes 1348
  2.0 194.8 %copy-start.3 = (s32[112]{0:T(128)S(1)}, s32[112]{0:T(128)}, u32[]{:S(2)}) copy-start(s32[112]{0:T(128)} %param.12) | copy-start | bytes 1348

commit v3 on v2

--- a/solution.py
+++ b/solution.py
@@ -462,7 +462,9 @@
             total = total + jnp.dot(pick, q_ref[:, b * V:(b + 1) * V], preferred_element_type=F32)
         snd[pl.ds(c * PER, PER)] = total.astype(BF16).reshape(PER, 16, V)
 
-    def send_chunk(c):
+    EIGHT = OWNERS // 8
+
+    def send(e):
         def step(o, carry):
             dz, dx = offset(o)
             peer = cluster_peer(dz, dx)
@@ -470,7 +472,7 @@
             copy(snd.at[o], rcv.at[o], d_send, d_recv.at[o // PER], peer).start()
             return carry
 
-        lax.fori_loop(1 if c == 0 else c * PER, (c + 1) * PER, step, 0)
+        lax.fori_loop(1 if e == 0 else e * EIGHT, (e + 1) * EIGHT, step, 0)
 
     def right(k):
         one = og.at[(z - k + 1 + NZ) % NZ]
@@ -490,7 +492,28 @@
         if k < 8:
             left(k).start()
 
+    def spread():
+        i, j = iota((8 * POOL, OWNERS * 16), 0), iota((8 * POOL, OWNERS * 16), 1)
+        at = i & 127
+        order = onehot(j == (at >> 5) * (NZ * 16) + (at & 15) * 16 + ((at >> 4) & 1) * 8 + (i >> 7))
+        for pair in range(2):
+            flat = jnp.concatenate(
+                [gp[2 * pair].reshape(OWNERS * 16, 128), gp[2 * pair + 1].reshape(OWNERS * 16, 128)], axis=1
+            )
+            part = jnp.dot(order, flat, preferred_element_type=F32).astype(BF16)
+            for cb in range(8):
+                for one in range(2):
+                    col = (2 * pair + one) * W + cb * 128
+                    pool[:, col:col + 128] = part[cb * 128:(cb + 1) * 128, one * 128:(one + 1) * 128]
+
+    def gather_facts(k, carry):
+        source = iota((128, NZ * RING), 0)
+        shift = onehot((iota((128, NZ * RING), 1) == source + k * RING) & (source < RING))
+        return carry + jnp.dot(tg[k].astype(BF16), shift, preferred_element_type=F32)
+
     gp[y, x, z] = piece_ref[y]
+    build(0)
+    build(1)
     pl.semaphore_wait(barrier, OWNERS - 1 + 7)
     ring(1)
 
@@ -500,53 +523,32 @@
         return carry
 
     lax.fori_loop(1, NZ, early, 0)
-    build(0)
-    send_chunk(0)
-    build(1)
+    send(0)
     ring(2)
+    send(1)
+    build(2)
+    ring(3)
+    send(2)
     some = gp.at[y, x, pl.ds(0, NZ - 1)]
     copy(some, some, p_send.at[0], p_recv.at[0], here).wait()
     for k in range(1, NX):
         copy(gp.at[y, x], gp.at[y, x], p_send.at[1], p_recv.at[1], cluster_peer(0, k)).start()
-    ring(3)
-    send_chunk(1)
-    build(2)
+    build(3)
     ring(4)
+    send(3)
+
+    some = tg.at[pl.ds(0, NZ - 1)]
+    copy(some, some, t_send.at[3], t_recv.at[3], here).wait()
+    span = NZ * RING
+    known = lax.fori_loop(0, NZ // 2, gather_facts, jnp.zeros((8, span), F32))
+    ring(5)
+    send(4)
+    known = lax.fori_loop(NZ // 2, NZ, gather_facts, known)
     some = gp.at[y, pl.ds(0, NX - 1)]
     copy(some, some, p_send.at[1], p_recv.at[1], here).wait()
     for k in range(1, NY):
         copy(gp.at[y], gp.at[y], p_send.at[2], p_recv.at[2], group_peer((y + k) % NY, core)).start()
-    ring(5)
-    send_chunk(2)
-    build(3)
     ring(6)
-    rcv[0] = snd[0]
-    mrcv[0] = msnd[0]
-    some = gp.at[pl.ds(0, NY - 1)]
-    copy(some, some, p_send.at[2], p_recv.at[2], here).wait()
-
-    def spread(yy, carry):
-        flat = gp[yy].reshape(OWNERS * 16, 128)
-        i, j = iota((POOL, OWNERS * 16), 0), iota((POOL, OWNERS * 16), 1)
-        base = (i >> 5) * (NZ * 16) + (i & 15) * 16 + ((i >> 4) & 1) * 8
-        for cb in range(8):
-            part = jnp.dot(onehot(j == base + cb), flat, preferred_element_type=F32).astype(BF16)
-            pool[:, pl.ds(pl.multiple_of(yy * W + cb * 128, 128), 128)] = part
-        return carry
-
-    some = tg.at[pl.ds(0, NZ - 1)]
-    copy(some, some, t_send.at[3], t_recv.at[3], here).wait()
-
-    ring(7)
-    send_chunk(3)
-    lax.fori_loop(0, NY, spread, 0)
-
-    def gather_facts(k, carry):
-        shift = onehot((iota((128, NZ * RING), 1) == iota((128, NZ * RING), 0) + k * RING) & (iota((128, NZ * RING), 0) < RING))
-        return carry + jnp.dot(tg[k].astype(BF16), shift, preferred_element_type=F32)
-
-    span = NZ * RING
-    known = lax.fori_loop(0, NZ, gather_facts, jnp.zeros((8, span), F32))
     dest = known[0:1].astype(jnp.int32)
     local = (known[4:5] > 0.5) & ((dest >> 2) == z)
     across = iota((1, span), 1)
@@ -556,6 +558,7 @@
     before = onehot(iota((span, span), 0) < across - block_of * SPARE)
     ranks = jnp.dot(onehot(mark), before, preferred_element_type=F32)
     order = jnp.sum(jnp.where(iota((8, span), 0) == to_x, ranks, 0.0), axis=0, keepdims=True).astype(jnp.int32)
+    ring(7)
     key = jnp.where(local, to_x * (4 * LATE) + block_of * LATE + order, -1)
     first_key = jnp.where(local & (block_of == 0), to_x * LATE + order, -1)
     key_col = jnp.broadcast_to(key.astype(F32), (8, span)).T[:, 0:1].astype(jnp.int32)
@@ -564,16 +567,26 @@
         preferred_element_type=F32,
     )
     ring(8)
+    rcv[0] = snd[0]
+    mrcv[0] = msnd[0]
     one = og.at[(z + 8) % NZ]
     copy(one, one, f_send.at[0], fr_recv.at[7], here).wait_recv()
-    for to in range(NX):
-        pick = onehot(iota((4 * LATE, span), 0) + to * (4 * LATE) == key)
-        px[to] = jnp.dot(pick, og[...].reshape(span, W), preferred_element_type=F32).astype(BF16)
+    send(5)
+    send(6)
+    send(7)
+    pick = onehot(iota((NX * 4 * LATE, span), 0) == key)
+    for ct in range(4):
+        cols = slice(ct * 256, (ct + 1) * 256)
+        part = jnp.dot(pick, og[:, :, cols].reshape(span, 256), preferred_element_type=F32).astype(BF16)
+        px[:, :, cols] = part.reshape(NX, 4 * LATE, 256)
     for k in range(1, NX):
         copy(px.at[(x + k) % NX], pv.at[x], x_send.at[0], x_recv.at[0], cluster_peer(0, k)).start()
         copy(pts, ptr.at[x], x_send.at[1], x_recv.at[1], cluster_peer(0, k)).start()
     pv[x] = px[x]
     ptr[x] = pts[...]
+    some = gp.at[pl.ds(0, NY - 1)]
+    copy(some, some, p_send.at[2], p_recv.at[2], here).wait()
+    spread()
 
     i, j = iota((256, 256), 0), iota((256, 256), 1)
     unmix = onehot(((i >> 1) & 15) * 16 + (i >> 5) * 2 + (i & 1) == j)
@@ -651,18 +664,18 @@
             gsnd[pl.ds((2 * h + c) * PER, PER)] = mixed.reshape(PER, 16, V)
         return sums
 
-    def send_back(c):
+    def send_back(e):
         def back(o, carry):
             dz, dx = offset(o)
             copy(gsnd.at[o], grcv.at[o], g_send, g_recv.at[o // PER], cluster_peer(-dz, -dx)).start()
             return carry
 
-        lax.fori_loop(1 if c == 0 else c * PER, (c + 1) * PER, back, 0)
+        lax.fori_loop(1 if e == 0 else e * EIGHT, (e + 1) * EIGHT, back, 0)
 
     sums = (jnp.zeros((1, 1), F32), jnp.zeros((1, 1), F32))
     sums = half(0, sums)
-    send_back(0)
-    send_back(1)
+    for e in range(4):
+        send_back(e)
     grcv[0] = gsnd[0]
 
     some = pv.at[pl.ds(0, NX - 1)]
@@ -684,14 +697,14 @@
     for k in range(1, NX):
         copy(rsn.at[(x + k) % NX], rv.at[x], x_send.at[2], x_recv.at[2], cluster_peer(0, k)).start()
     rv[x] = rsn[x]
-    sums = half(1, sums)
 
     some = rv.at[pl.ds(0, NX - 1)]
     copy(some, some, x_send.at[2], x_recv.at[2], here).wait()
-    cols_iota = iota((RING, NX * 4 * LATE), 1)
-    for k in range(NZ):
-        pick = onehot(cols_iota == key_col[k * RING:(k + 1) * RING])
-        cc[k] = jnp.dot(pick, rv[...].reshape(NX * 4 * LATE, W), preferred_element_type=F32).astype(BF16)
+    pick = onehot(iota((span, NX * 4 * LATE), 1) == key_col)
+    for ct in range(4):
+        cols = slice(ct * 256, (ct + 1) * 256)
+        part = jnp.dot(pick, rv[:, :, cols].reshape(NX * 4 * LATE, 256), preferred_element_type=F32).astype(BF16)
+        cc[:, :, cols] = part.reshape(NZ, RING, 256)
 
     def ring_back(k):
         to = (z + 9 - k) % NZ
@@ -707,7 +720,9 @@
             copy(cc.at[to], ll.at[k - 1], b_send.at[1], bl_recv.at[k - 1], cluster_peer(-1, 0)).start()
 
     ring_back(1)
-    send_back(2)
+    sums = half(1, sums)
+    ring_back(2)
+    send_back(4)
 
     low[:, TP:256] = jnp.zeros((256, 256 - TP), F32)
     lowt[...] = low[...].T.astype(BF16)
@@ -731,8 +746,8 @@
     ]
     for one in move:
         one.start()
-    ring_back(2)
-    send_back(3)
+    ring_back(3)
+    send_back(5)
 
     def passage_term(k, carry):
         cols = pl.ds(pl.multiple_of(k * 512, 512), 512)
@@ -740,7 +755,10 @@
         pg_ref[:, cols] = (factor * part).astype(BF16)
         return carry
 
-    lax.fori_loop(0, 8, passage_term, 0)
+    lax.fori_loop(0, 4, passage_term, 0)
+    ring_back(4)
+    send_back(6)
+    lax.fori_loop(4, 8, passage_term, 0)
     for one in move:
         one.wait()
     s1[...] = pt[core] + rc[...]
@@ -750,7 +768,8 @@
         to = (y + k) % NY
         copy(s1.at[to], ry.at[k - 1], r_send.at[1], r_recv.at[1], group_peer(to, core)).start()
         copy(sc.at[1], rys.at[k - 1], t_send.at[1], t_recv.at[1], group_peer(to, core)).start()
-    ring_back(3)
+    ring_back(5)
+    send_back(7)
     copy(ry, ry, r_send.at[1], r_recv.at[1], here).wait()
     copy(rys, rys, t_send.at[1], t_recv.at[1], here).wait()
     s2[...] = (s1[y] + ry[0] + ry[1] + ry[2]).reshape(NX, 32, 512)
@@ -760,7 +779,7 @@
         to = (x + k) % NX
         copy(s2.at[to], rx.at[k - 1], r_send.at[2], r_recv.at[2], cluster_peer(0, k)).start()
         copy(sc.at[2], rxs.at[k - 1], t_send.at[2], t_recv.at[2], cluster_peer(0, k)).start()
-    ring_back(4)
+    ring_back(6)
     copy(rx, rx, r_send.at[2], r_recv.at[2], here).wait()
     copy(rxs, rxs, t_send.at[2], t_recv.at[2], here).wait()
     s3 = s2[x] + rx[0] + rx[1] + rx[2]
@@ -775,8 +794,7 @@
         return carry
 
     lax.fori_loop(1, NZ, to_z, 0)
-    ring_back(5)
-    ring_back(6)
+    ring_back(7)
     copy(rz, rz, r_send.at[3], r_recv.at[3], here).wait()
     last = zb[z] + jnp.sum(rz[...], axis=0)
     fin[...] = last[0:8]
@@ -790,23 +808,22 @@
         return carry
 
     lax.fori_loop(1, 8, to_group, 0)
-    ring_back(7)
+    ring_back(8)
 
     def take(c):
         some = bundles(grcv, c)
         copy(some, some, g_send, g_recv.at[c], here).wait_recv()
         rows = grcv[pl.ds(c * PER, PER)].reshape(PER * 16, V)
         lanes = iota((TQ, PER * 16), 1) + c * (PER * 16)
+        pick = jnp.concatenate([onehot(lanes == place_col + BASE * b) for b in range(8)], axis=0)
+        part = jnp.dot(pick, rows, preferred_element_type=F32)
         for b in range(8):
-            part = jnp.dot(onehot(lanes == place_col + BASE * b), rows, preferred_element_type=F32)
             if c == 0:
-                acc[:, b * V:(b + 1) * V] = part
+                acc[:, b * V:(b + 1) * V] = part[b * TQ:(b + 1) * TQ]
             else:
-                acc[:, b * V:(b + 1) * V] += part
-
-    take(0)
-    ring_back(8)
-    for c in range(1, CHUNKS):
+                acc[:, b * V:(b + 1) * V] += part[b * TQ:(b + 1) * TQ]
+
+    for c in range(CHUNKS):
         take(c)
     copy(rr.at[7], rr.at[7], b_send.at[0], br_recv.at[7], here).wait_recv()
     copy(ll.at[6], ll.at[6], b_send.at[1], bl_recv.at[6], here).wait_recv()

time: 206 us -> 188 us (0.913)
  Pallas kernels: 194 us -> 177 us
    pallas_call x1, Pallas kernels: 194 us -> 177 us  [fast_call(): pl.pallas_call(fast_kernel, out_shape=(jax.ShapeDtypeStruct((TQ, D), BF16...]
where the time goes in v3:
time: 188 us; the launch traced here: 186 us
  Pallas kernels  177 us (94%)
  between operations  5.47 us (3%)
  local copies, waits for them, and re-layouts  3.42 us (2%)
    pallas_call x1, Pallas kernels, fast_call(): pl.pallas_call(fast_kernel, out_shape=(jax.ShapeDtypeStruct((TQ, D), BF16...  177 us

profile of v3, /device:TPU:1, one launch (start us, length us, event | category | flops | bytes accessed | tf_op | source)
XLA Modules:
  0.0 186.5 jit_solution(17242202958945721458)
XLA Ops:
  1.3 0.7 copy_bitcast_fusion.1.piece_ref
  2.0 0.0 copy-start
  2.0 0.0 copy-start.1
  2.0 0.0 copy-start.2
  2.0 0.0 copy-start.3
  2.0 177.4 %shard_map.120 = (bf16[112,4096]{1,0:T(8,128)(2,1)S(1)}, bf16[192,4096]{1,0:T(8,128)(2,1)S(1)}, f32[2,4096]{1,0:T(2,128)S(1)}, f32[1]{0:T(128)}, f32[1]{0:T(128)}, /*index=5*/f32[1]{0:T(128)}) custom-call(bf16[112,4096]{1,0:T(8,128)(2,1)} %q_ref.1, s32[1,112]{1,0:T(1,128)} %bitcast.16, s32[2,112]{1,0:T(2,128)} %bitcast.14, s32[1,112]{1,0:T(1,128)} %bitcast.18, ...), custom_call_target="tpu_custom_call" | custom-call | flops 4000000000 | bytes 6000000 | tf_op jit(solution)/shard_map/pallas_call | solution.py:883
  180.0 0.0 copy-done
  180.0 0.0 copy-done.1
  180.0 0.0 copy-done.2
  180.1 0.0 copy-done.3
  180.1 0.2 conditional.1
  180.3 0.9 copy.43
  181.2 1.1 copy.44
  182.4 0.6 copy.45
Async XLA Ops:
  2.0 178.0 %copy-start = (bf16[112,4096]{1,0:T(8,128)(2,1)S(1)}, bf16[112,4096]{1,0:T(8,128)(2,1)}, u32[]{:S(2)}) copy-start(bf16[112,4096]{1,0:T(8,128)(2,1)} %q_ref.1) | copy-start | bytes 2752516
  2.0 178.0 %copy-start.1 = (s32[112,2]{0,1:T(2,128)S(1)}, s32[112,2]{0,1:T(2,128)}, u32[]{:S(2)}) copy-start(s32[112,2]{0,1:T(2,128)} %param.11) | copy-start | bytes 2692
  2.0 178.0 %copy-start.2 = (s32[112,1]{0,1:T(1,128)S(1)}, s32[112,1]{0,1:T(1,128)}, u32[]{:S(2)}) copy-start(s32[112,1]{0,1:T(1,128)} %param.10) | copy-start | bytes 1348
  2.0 178.0 %copy-start.3 = (s32[112]{0:T(128)S(1)}, s32[112]{0:T(128)}, u32[]{:S(2)}) copy-start(s32[112]{0:T(128)} %param.12) | copy-start | bytes 1348

commit v4 on v3

--- a/solution.py
+++ b/solution.py
@@ -437,11 +437,14 @@
     meta = jnp.dot(onehot(iota((OWNERS, TQ), 0) == off_row), value, preferred_element_type=F32)
     msnd[:, 0, :] = meta
 
+    def spot_of(d):
+        return (d + 3) % NZ
+
     total = jnp.zeros((RING, W), F32)
     for b in range(4):
         pick = onehot(iota((RING, TQ), 0) == spare_row + SPARE * b)
         total = total + jnp.dot(pick, q_ref[:, b * W:(b + 1) * W], preferred_element_type=F32)
-    og[z] = total.astype(BF16)
+    og[spot_of(0)] = total.astype(BF16)
     kind = iota((8, TQ), 0)
     facts = jnp.where(
         kind == 0, cl_row.astype(F32),
@@ -452,7 +455,7 @@
     )
     facts = jnp.where(kind < 5, facts, 0.0).astype(BF16)
     spot = lane % SPARE
-    tg[z] = jnp.dot(facts, onehot((spot == spare_col) & (lane < RING)), preferred_element_type=F32)
+    tg[spot_of(0)] = jnp.dot(facts, onehot((spot == spare_col) & (lane < RING)), preferred_element_type=F32)
 
     def build(c):
         row = iota((PER * 16, TQ), 0) + c * (PER * 16)
@@ -474,23 +477,18 @@
 
         lax.fori_loop(1 if e == 0 else e * EIGHT, (e + 1) * EIGHT, step, 0)
 
-    def right(k):
-        one = og.at[(z - k + 1 + NZ) % NZ]
-        return copy(one, one, f_send.at[0], fr_recv.at[k - 1], cluster_peer(1, 0))
-
-    def left(k):
-        one = og.at[(z + k - 1) % NZ]
-        return copy(one, one, f_send.at[1], fl_recv.at[k - 1], cluster_peer(-1, 0))
-
     def ring(k):
         if k > 1:
-            one = og.at[(z - k + 1 + NZ) % NZ]
-            copy(one, one, f_send.at[0], fr_recv.at[k - 2], here).wait_recv()
-            one = og.at[(z + k - 1) % NZ]
+            if k <= 8:
+                one = og.at[0]
+                copy(one, one, f_send.at[0], fr_recv.at[k - 2], here).wait_recv()
+            one = og.at[0]
             copy(one, one, f_send.at[1], fl_recv.at[k - 2], here).wait_recv()
-        right(k).start()
         if k < 8:
-            left(k).start()
+            copy(
+                og.at[spot_of(1 - k)], og.at[spot_of(-k)], f_send.at[0], fr_recv.at[k - 1], cluster_peer(1, 0)
+            ).start()
+        copy(og.at[spot_of(k - 1)], og.at[spot_of(k)], f_send.at[1], fl_recv.at[k - 1], cluster_peer(-1, 0)).start()
 
     def spread():
         i, j = iota((8 * POOL, OWNERS * 16), 0), iota((8 * POOL, OWNERS * 16), 1)
@@ -518,7 +516,7 @@
     ring(1)
 
     def early(k, carry):
-        copy(tg.at[z], tg.at[z], t_send.at[3], t_recv.at[3], cluster_peer(k, 0)).start()
+        copy(tg.at[spot_of(0)], tg.at[(19 - k) % NZ], t_send.at[3], t_recv.at[3], cluster_peer(k, 0)).start()
         copy(gp.at[y, x, z], gp.at[y, x, z], p_send.at[0], p_recv.at[0], cluster_peer(k, 0)).start()
         return carry
 
@@ -553,37 +551,48 @@
     local = (known[4:5] > 0.5) & ((dest >> 2) == z)
     across = iota((1, span), 1)
     block_of = (across % RING) // SPARE
+    part_of = jnp.where(across >= span // 2, 1, 0)
     to_x = dest & 3
-    mark = (iota((8, span), 0) == to_x) & local & (block_of == 0)
+    mark = (iota((8, span), 0) == part_of * NX + to_x) & local & (block_of == 0)
     before = onehot(iota((span, span), 0) < across - block_of * SPARE)
     ranks = jnp.dot(onehot(mark), before, preferred_element_type=F32)
-    order = jnp.sum(jnp.where(iota((8, span), 0) == to_x, ranks, 0.0), axis=0, keepdims=True).astype(jnp.int32)
-    ring(7)
-    key = jnp.where(local, to_x * (4 * LATE) + block_of * LATE + order, -1)
-    first_key = jnp.where(local & (block_of == 0), to_x * LATE + order, -1)
+    order = jnp.sum(jnp.where(iota((8, span), 0) == part_of * NX + to_x, ranks, 0.0), axis=0, keepdims=True).astype(jnp.int32)
+    key = jnp.where(local, to_x * (4 * NZ) + block_of * NZ + order, -1)
+    first_key = jnp.where(local & (block_of == 0), to_x * LATE + part_of * NZ + order, -1)
     key_col = jnp.broadcast_to(key.astype(F32), (8, span)).T[:, 0:1].astype(jnp.int32)
     pts[...] = lax.dot_general(
         known.astype(BF16), onehot(iota((NX * LATE, span), 0) == first_key), (((1,), (1,)), ((), ())),
         preferred_element_type=F32,
     )
-    ring(8)
+
+    MIX = NX * 4 * NZ
+    HS = span // 2
+
+    def hand_on(h):
+        pick = onehot(iota((MIX, HS), 0) == key[:, h * HS:(h + 1) * HS])
+        for ct in range(2):
+            cols = slice(ct * 512, (ct + 1) * 512)
+            held = og[h * 8:(h + 1) * 8, :, cols].reshape(HS, 512)
+            part = jnp.dot(pick, held, preferred_element_type=F32).astype(BF16)
+            px[h, :, :, cols] = part.reshape(NX, 4 * NZ, 512)
+        for k in range(1, NX):
+            copy(px.at[h, (x + k) % NX], pv.at[h, x], x_send.at[h], x_recv.at[h], cluster_peer(0, k)).start()
+        pv[h, x] = px[h, x]
+
+    hand_on(0)
+    for k in range(1, NX):
+        copy(pts, ptr.at[x], x_send.at[2], x_recv.at[2], cluster_peer(0, k)).start()
+    ptr[x] = pts[...]
+    ring(7)
     rcv[0] = snd[0]
     mrcv[0] = msnd[0]
-    one = og.at[(z + 8) % NZ]
-    copy(one, one, f_send.at[0], fr_recv.at[7], here).wait_recv()
+    ring(8)
     send(5)
+    one = og.at[0]
+    copy(one, one, f_send.at[1], fl_recv.at[7], here).wait_recv()
+    hand_on(1)
     send(6)
     send(7)
-    pick = onehot(iota((NX * 4 * LATE, span), 0) == key)
-    for ct in range(4):
-        cols = slice(ct * 256, (ct + 1) * 256)
-        part = jnp.dot(pick, og[:, :, cols].reshape(span, 256), preferred_element_type=F32).astype(BF16)
-        px[:, :, cols] = part.reshape(NX, 4 * LATE, 256)
-    for k in range(1, NX):
-        copy(px.at[(x + k) % NX], pv.at[x], x_send.at[0], x_recv.at[0], cluster_peer(0, k)).start()
-        copy(pts, ptr.at[x], x_send.at[1], x_recv.at[1], cluster_peer(0, k)).start()
-    pv[x] = px[x]
-    ptr[x] = pts[...]
     some = gp.at[pl.ds(0, NY - 1)]
     copy(some, some, p_send.at[2], p_recv.at[2], here).wait()
     spread()
@@ -678,14 +687,17 @@
         send_back(e)
     grcv[0] = gsnd[0]
 
-    some = pv.at[pl.ds(0, NX - 1)]
-    copy(some, some, x_send.at[0], x_recv.at[0], here).wait()
+    for h in range(2):
+        some = pv.at[h, pl.ds(0, NX - 1)]
+        copy(some, some, x_send.at[h], x_recv.at[h], here).wait()
     some = ptr.at[pl.ds(0, NX - 1)]
-    copy(some, some, x_send.at[1], x_recv.at[1], here).wait()
+    copy(some, some, x_send.at[2], x_recv.at[2], here).wait()
     choose = onehot(iota((LATE, 128), 1) == iota((LATE, 128), 0) + x * LATE)
     for via in range(NX):
-        for b in range(4):
-            routed[128 + via * LATE:128 + (via + 1) * LATE, b * W:(b + 1) * W] = pv[via, b * LATE:(b + 1) * LATE, :]
+        for h in range(2):
+            lo = 128 + via * LATE + h * NZ
+            for b in range(4):
+                routed[lo:lo + NZ, b * W:(b + 1) * W] = pv[h, via, b * NZ:(b + 1) * NZ, :]
         late[via * LATE:(via + 1) * LATE, 0:8] = lax.dot_general(
             choose, ptr[via].astype(BF16), contract, preferred_element_type=F32
         )
@@ -693,35 +705,42 @@
     for b in range(4):
         part = grads(slice(b * W, (b + 1) * W))
         for via in range(NX):
-            rsn[via, b * LATE:(b + 1) * LATE, :] = part[via * LATE:(via + 1) * LATE]
-    for k in range(1, NX):
-        copy(rsn.at[(x + k) % NX], rv.at[x], x_send.at[2], x_recv.at[2], cluster_peer(0, k)).start()
-    rv[x] = rsn[x]
-
-    some = rv.at[pl.ds(0, NX - 1)]
-    copy(some, some, x_send.at[2], x_recv.at[2], here).wait()
-    pick = onehot(iota((span, NX * 4 * LATE), 1) == key_col)
-    for ct in range(4):
-        cols = slice(ct * 256, (ct + 1) * 256)
-        part = jnp.dot(pick, rv[:, :, cols].reshape(NX * 4 * LATE, 256), preferred_element_type=F32).astype(BF16)
-        cc[:, :, cols] = part.reshape(NZ, RING, 256)
+            for h in range(2):
+                lo = via * LATE + h * NZ
+                rsn[h, via, b * NZ:(b + 1) * NZ, :] = part[lo:lo + NZ]
+    for h in (1, 0):
+        for k in range(1, NX):
+            copy(rsn.at[h, (x + k) % NX], rv.at[h, x], x_send.at[3 + h], x_recv.at[3 + h], cluster_peer(0, k)).start()
+        rv[h, x] = rsn[h, x]
+
+    def share(h):
+        some = rv.at[h, pl.ds(0, NX - 1)]
+        copy(some, some, x_send.at[3 + h], x_recv.at[3 + h], here).wait()
+        pick = onehot(iota((HS, MIX), 1) == key_col[h * HS:(h + 1) * HS])
+        for ct in range(2):
+            cols = slice(ct * 512, (ct + 1) * 512)
+            back = rv[h, :, :, cols].reshape(MIX, 512)
+            part = jnp.dot(pick, back, preferred_element_type=F32).astype(BF16)
+            cc[h * 8:(h + 1) * 8, :, cols] = part.reshape(8, RING, 512)
+
+    share(1)
 
     def ring_back(k):
-        to = (z + 9 - k) % NZ
+        to = spot_of(9 - k)
         if k > 1:
             copy(rr.at[k - 2], rr.at[k - 2], b_send.at[0], br_recv.at[k - 2], here).wait_recv()
             cc[to] = cc[to] + rr[k - 2]
         copy(cc.at[to], rr.at[k - 1], b_send.at[0], br_recv.at[k - 1], cluster_peer(1, 0)).start()
         if k < 8:
-            to = (z - 8 + k + NZ) % NZ
+            to = spot_of(k - 8)
             if k > 1:
                 copy(ll.at[k - 2], ll.at[k - 2], b_send.at[1], bl_recv.at[k - 2], here).wait_recv()
                 cc[to] = cc[to] + ll[k - 2]
             copy(cc.at[to], ll.at[k - 1], b_send.at[1], bl_recv.at[k - 1], cluster_peer(-1, 0)).start()
 
     ring_back(1)
+    ring_back(2)
     sums = half(1, sums)
-    ring_back(2)
     send_back(4)
 
     low[:, TP:256] = jnp.zeros((256, 256 - TP), F32)
@@ -748,6 +767,7 @@
         one.start()
     ring_back(3)
     send_back(5)
+    share(0)
 
     def passage_term(k, carry):
         cols = pl.ds(pl.multiple_of(k * 512, 512), 512)
@@ -827,7 +847,7 @@
         take(c)
     copy(rr.at[7], rr.at[7], b_send.at[0], br_recv.at[7], here).wait_recv()
     copy(ll.at[6], ll.at[6], b_send.at[1], bl_recv.at[6], here).wait_recv()
-    spare_rows = cc[z] + rr[7] + ll[6]
+    spare_rows = cc[spot_of(0)] + rr[7] + ll[6]
     for b in range(4):
         pick = onehot(iota((TQ, RING), 1) == spare_col + SPARE * b)
         part = jnp.dot(pick, spare_rows, preferred_element_type=F32)
@@ -847,7 +867,7 @@
     some = mrcv.at[pl.ds(1, OWNERS - 1)]
     copy(some, some, m_send, m_recv.at[0], here).wait_send()
     for side, count in ((0, 8), (1, 7)):
-        some = og.at[pl.ds(0, count)]
+        some = og.at[pl.ds(0, 15 - count)]
         copy(some, some, f_send.at[side], fr_recv.at[0], here).wait_send()
         some = cc.at[pl.ds(0, count)]
         copy(some, some, b_send.at[side], br_recv.at[0], here).wait_send()
@@ -877,7 +897,7 @@
     sm = pl.BlockSpec(memory_space=pltpu.SMEM)
     bundle = pltpu.VMEM((OWNERS, 16, V), BF16)
     note = pltpu.VMEM((OWNERS, 1, 128), F32)
-    column = pltpu.VMEM((NX, 4 * LATE, W), BF16)
+    column = pltpu.VMEM((2, NX, 4 * NZ, W), BF16)
     dma = pltpu.SemaphoreType.DMA
     scalar = jax.ShapeDtypeStruct((1,), F32)
     return pl.pallas_call(
@@ -912,7 +932,7 @@
             *reduce_scratch(),
             dma, dma((CHUNKS,)), dma, dma((CHUNKS,)), dma, dma((CHUNKS,)),
             dma((3,)), dma((3,)), dma((5,)), dma((5,)), dma((4,)), dma((4,)),
-            dma((2,)), dma((8,)), dma((7,)), dma((2,)), dma((8,)), dma((7,)), dma((3,)), dma((3,)),
+            dma((2,)), dma((7,)), dma((8,)), dma((2,)), dma((8,)), dma((7,)), dma((5,)), dma((5,)),
         ],
         compiler_params=pltpu.CompilerParams(
             collective_id=1, has_side_effects=True, vmem_limit_bytes=48 * 1024 * 1024

time: 188 us -> 184 us (0.979)
  Pallas kernels: 177 us -> 174 us
    pallas_call x1, Pallas kernels: 177 us -> 174 us  [fast_call(): pl.pallas_call(fast_kernel, out_shape=(jax.ShapeDtypeStruct((TQ, D), BF16...]
where the time goes in v4:
time: 184 us; the launch traced here: 183 us
  Pallas kernels  174 us (95%)
  between operations  5.47 us (3%)
  local copies, waits for them, and re-layouts  3.42 us (2%)
    pallas_call x1, Pallas kernels, fast_call(): pl.pallas_call(fast_kernel, out_shape=(jax.ShapeDtypeStruct((TQ, D), BF16...  174 us

profile of v4, /device:TPU:1, one launch (start us, length us, event | category | flops | bytes accessed | tf_op | source)
XLA Modules:
  0.0 183.0 jit_solution(17362445005536494722)
XLA Ops:
  1.3 0.7 copy_bitcast_fusion.1.piece_ref
  2.0 0.0 copy-start
  2.0 0.0 copy-start.1
  2.0 0.0 copy-start.2
  2.0 0.0 copy-start.3
  2.0 174.0 %shard_map.120 = (bf16[112,4096]{1,0:T(8,128)(2,1)S(1)}, bf16[192,4096]{1,0:T(8,128)(2,1)S(1)}, f32[2,4096]{1,0:T(2,128)S(1)}, f32[1]{0:T(128)}, f32[1]{0:T(128)}, /*index=5*/f32[1]{0:T(128)}) custom-call(bf16[112,4096]{1,0:T(8,128)(2,1)} %q_ref.1, s32[1,112]{1,0:T(1,128)} %bitcast.16, s32[2,112]{1,0:T(2,128)} %bitcast.14, s32[1,112]{1,0:T(1,128)} %bitcast.18, ...), custom_call_target="tpu_custom_call" | custom-call | flops 4000000000 | bytes 6000000 | tf_op jit(solution)/shard_map/pallas_call | solution.py:903
  176.6 0.0 copy-done
  176.6 0.0 copy-done.1
  176.6 0.0 copy-done.2
  176.6 0.0 copy-done.3
  176.7 0.2 conditional.1
  176.8 0.9 copy.43
  177.8 1.1 copy.44
  178.9 0.6 copy.45
Async XLA Ops:
  2.0 174.6 %copy-start = (bf16[112,4096]{1,0:T(8,128)(2,1)S(1)}, bf16[112,4096]{1,0:T(8,128)(2,1)}, u32[]{:S(2)}) copy-start(bf16[112,4096]{1,0:T(8,128)(2,1)} %q_ref.1) | copy-start | bytes 2752516
  2.0 174.6 %copy-start.1 = (s32[112,2]{0,1:T(2,128)S(1)}, s32[112,2]{0,1:T(2,128)}, u32[]{:S(2)}) copy-start(s32[112,2]{0,1:T(2,128)} %param.11) | copy-start | bytes 2692
  2.0 174.6 %copy-start.2 = (s32[112,1]{0,1:T(1,128)S(1)}, s32[112,1]{0,1:T(1,128)}, u32[]{:S(2)}) copy-start(s32[112,1]{0,1:T(1,128)} %param.10) | copy-start | bytes 1348
  2.0 174.6 %copy-start.3 = (s32[112]{0:T(128)S(1)}, s32[112]{0:T(128)}, u32[]{:S(2)}) copy-start(s32[112]{0:T(128)} %param.12) | copy-start | bytes 1348
